TPU v7x, 256 devices: a whole 4x4x8 slice. The times are simulated.
256 devices in a mesh: table: 64 (over y, x, z_lo, core), rep: 4 (over z_hi).
Axes of the slice: x: 4, y: 4, z: 8 (z_hi: 4, z_lo: 2; z = z_hi * 2 + z_lo), core: 2. Of those that a mesh axis runs over, the one named last changes fastest.
Arguments:
- pooled: bfloat16 [2048, 32768], P('rep', 'table'), may hold values from -6 to 6
- table_slot: int32 [256], replicated, may hold values from 0 to 255, each once
- cross_v: bfloat16 [32768, 256], P('table'), may hold values from -0.03125 to 0.03125
- cross_u: bfloat16 [256, 32768], P(None, 'table'), may hold values from -0.375 to 0.375
- cross_bias: float32 [32768], P('table'), may hold values from -3 to 3
- block_index1: int32 [256], replicated, may hold values from 0 to 255, each once
- weight1: bfloat16 [256, 128, 128], P('table'), may hold values from -0.1875 to 0.1875
- block_index2: int32 [128], replicated, may hold values from 0 to 31
- weight2: bfloat16 [128, 128, 128], P('table'), may hold values from -0.25 to 0.25
- top_vectors: float32 [3, 4096], replicated, may hold values from -0.6 to 0.6
- labels: int32 [4, 512], P('rep', 'table'), may hold values 0 or 1
- importance: int32 [4, 512], P('rep', 'table'), may hold values from 1 to 16
Outputs:
- d_pooled: bfloat16 [2048, 32768], P('rep', 'table')
- grad_v: float32 [32768, 256], P('table')
- grad_u: float32 [256, 32768], P(None, 'table')
- grad_bias: float32 [32768], P('table')
- grad_w1: float32 [256, 128, 128], P('table')
- grad_w2: float32 [128, 128, 128], P('table')
- grad_vectors: float32 [3, 4096], replicated
All inputs are finite; a program needn't handle non-finite values. No bound on the sum of `labels` on one device may be relied on, other than what follows from the above.
Results may differ from a plain program's by a relative error of at most 0.024.
Values may be sent and summed in bfloat16 or wider, within the bound.
No kernel may reach another device: no remote copies, remote signals or barrier semaphores. Data moves between devices by JAX's collectives and lax.ppermute only.
A program may use at most 128 MiB of HBM per device.

v0:
```python
import jax
import jax.numpy as jnp
from jax import lax
from jax.sharding import PartitionSpec as P

E = 128
K2 = 4
HB = 32


def silu_slope(value):
    squash = jax.nn.sigmoid(value)
    return squash * (1.0 + value * (1.0 - squash))


def block_forward(blocks, columns, weight, per_column, offset):
    batch_rows = blocks.shape[0]
    picked = blocks[:, columns]
    block_terms = jnp.einsum("bnc,ncd->bnd", picked, weight, preferred_element_type=jnp.float32)
    summed = block_terms.reshape(batch_rows, -1, per_column, E).sum(axis=2)
    return (summed + offset.reshape(-1, E), picked)


def body(
    pooled,
    table_slot,
    cross_v,
    cross_u,
    cross_bias,
    block_index1,
    weight1,
    block_index2,
    weight2,
    top_vectors,
    labels,
    importance,
):
    tables = table_slot.shape[0]
    per_first = tables // HB
    contract_last = (((1,), (1,)), ((), ()))
    contract_first = (((0,), (0,)), ((), ()))
    partial_sum = jnp.dot(pooled, cross_v, preferred_element_type=jnp.float32)
    crossed = lax.psum(partial_sum, "table").astype(jnp.bfloat16)
    factor = jnp.dot(crossed, cross_u, preferred_element_type=jnp.float32) + cross_bias + 1.0
    lifted = (pooled.astype(jnp.float32) * factor).astype(jnp.bfloat16)
    sample_rows = lax.all_to_all(lifted, "table", split_axis=0, concat_axis=1, tiled=True)
    batch_rows = sample_rows.shape[0]
    lifted_blocks = sample_rows.reshape(batch_rows, tables, E)
    slot_of = (
        jnp.zeros((tables,), jnp.int32).at[table_slot].set(jnp.arange(tables, dtype=jnp.int32))
    )
    columns_one = slot_of[block_index1]
    full_one, full_two = (
        lax.all_gather(weight1, "table", axis=0, tiled=True),
        lax.all_gather(weight2, "table", axis=0, tiled=True),
    )
    preact_one, picked_one = block_forward(
        lifted_blocks, columns_one, full_one, per_first, top_vectors[0]
    )
    hidden_one = jax.nn.silu(preact_one).astype(jnp.bfloat16)
    preact_two, picked_two = block_forward(hidden_one, block_index2, full_two, K2, top_vectors[1])
    hidden_two = jax.nn.silu(preact_two).astype(jnp.bfloat16)
    last_weight = top_vectors[2].reshape(-1, E)
    logit = jnp.sum(hidden_two.astype(jnp.float32) * last_weight, axis=(1, 2))
    sample_weight = importance.reshape(-1).astype(jnp.float32) / 8.0
    targets = labels.reshape(-1).astype(jnp.float32)
    grad_logit = sample_weight * (jax.nn.sigmoid(logit) - targets)
    grad_two = (grad_logit[:, None, None] * last_weight * silu_slope(preact_two)).astype(
        jnp.bfloat16
    )
    spread_two = jnp.repeat(grad_two, K2, axis=1)
    local_two = jnp.einsum(
        "bnc,bnd->ncd", picked_two, spread_two, preferred_element_type=jnp.float32
    )
    back_two = jnp.einsum("bnd,ncd->bnc", spread_two, full_two, preferred_element_type=jnp.float32)
    onehot_two = (block_index2[:, None] == jnp.arange(HB, dtype=jnp.int32)[None, :]).astype(
        jnp.float32
    )
    into_one = jnp.einsum("bnc,nj->bjc", back_two, onehot_two, precision=lax.Precision.HIGHEST)
    grad_one = (into_one * silu_slope(preact_one)).astype(jnp.bfloat16)
    spread_one = jnp.repeat(grad_one, per_first, axis=1)
    local_one = jnp.einsum(
        "bnc,bnd->ncd", picked_one, spread_one, preferred_element_type=jnp.float32
    )
    back_one = jnp.einsum("bnd,ncd->bnc", spread_one, full_one, preferred_element_type=jnp.float32)
    onehot_one = (columns_one[:, None] == jnp.arange(tables, dtype=jnp.int32)[None, :]).astype(
        jnp.float32
    )
    into_lifted = jnp.einsum("bnc,ns->bsc", back_one, onehot_one, precision=lax.Precision.HIGHEST)
    grad_lifted = into_lifted.reshape(batch_rows, -1).astype(jnp.bfloat16)
    vectors_local = jnp.stack(
        [
            jnp.sum(grad_one.astype(jnp.float32), axis=0).reshape(-1),
            jnp.sum(grad_two.astype(jnp.float32), axis=0).reshape(-1),
            jnp.sum(hidden_two.astype(jnp.float32) * grad_logit[:, None, None], axis=0).reshape(-1),
        ]
    )
    returned = lax.all_to_all(grad_lifted, "table", split_axis=1, concat_axis=0, tiled=True)
    cross_grad = returned.astype(jnp.float32) * pooled.astype(jnp.float32)
    cross_half = cross_grad.astype(jnp.bfloat16)
    direct = returned.astype(jnp.float32) * factor
    partial_back = lax.dot_general(
        cross_half, cross_u, contract_last, preferred_element_type=jnp.float32
    )
    grad_crossed = lax.psum(partial_back, "table").astype(jnp.bfloat16)
    local_u = lax.dot_general(
        crossed, cross_half, contract_first, preferred_element_type=jnp.float32
    )
    local_bias = jnp.sum(cross_grad, axis=0)
    local_v = lax.dot_general(
        pooled, grad_crossed, contract_first, preferred_element_type=jnp.float32
    )
    d_pooled = (
        direct
        + lax.dot_general(grad_crossed, cross_v, contract_last, preferred_element_type=jnp.float32)
    ).astype(jnp.bfloat16)
    summed_one, summed_two = (
        lax.psum_scatter(local_one, "table", scatter_dimension=0, tiled=True),
        lax.psum_scatter(local_two, "table", scatter_dimension=0, tiled=True),
    )
    grad_w1, grad_w2, grad_v, grad_u, grad_bias = (
        lax.psum(summed_one.astype(jnp.bfloat16), "rep").astype(jnp.float32),
        lax.psum(summed_two.astype(jnp.bfloat16), "rep").astype(jnp.float32),
        lax.psum(local_v.astype(jnp.bfloat16), "rep").astype(jnp.float32),
        lax.psum(local_u.astype(jnp.bfloat16), "rep").astype(jnp.float32),
        lax.psum(local_bias.astype(jnp.bfloat16), "rep").astype(jnp.float32),
    )
    grad_vectors = lax.psum(vectors_local, ("table", "rep"))
    return (d_pooled, grad_v, grad_u, grad_bias, grad_w1, grad_w2, grad_vectors)


def solution(mesh):
    placed = (
        P("rep", "table"),
        P(),
        P("table", None),
        P(None, "table"),
        P("table"),
        P(),
        P("table", None, None),
        P(),
        P("table", None, None),
        P(),
        P("rep", "table"),
        P("rep", "table"),
    )
    return jax.shard_map(
        body,
        mesh=mesh,
        in_specs=placed,
        out_specs=(
            P("rep", "table"),
            P("table", None),
            P(None, "table"),
            P("table"),
            P("table", None, None),
            P("table", None, None),
            P(),
        ),
        check_vma=False,
    )
```

profile of v0, /device:TPU:2, one launch (start us, length us, event | category | flops | bytes accessed | tf_op | source)
XLA Modules:
  0.0 1053.5 jit_solution(16839021764500228919)
XLA Ops:
  7.2 0.0 copy-start
  7.2 0.0 all-gather.3.cloned.1.call-start
  7.2 0.7 all-gather.3.cloned.1.call-update
  7.9 0.0 all-gather.5.cloned.1.call-start
  8.0 0.7 all-gather.5.cloned.1.call-update
  8.7 1.4 fusion.43
  10.1 273.2 %all-reduce.6 = bf16[512,256]{1,0:T(8,128)(2,1)S(1)} all-reduce(f32[512,256]{1,0:T(8,128)S(1)} %fusion.43), channel_id=1, replica_groups=mesh['table'=64,'rep'=4] {'table'}, use_global_device_ids=true, to_apply=%region_1.0 | all-reduce | flops 131072 | bytes 786432 | tf_op jit(solution)/shard_map/psum | solution.py:43
  283.3 0.0 copy-done
  283.3 1.0 fusion
  284.3 2.0 fusion.10
  286.3 15.7 %all-to-all-start = ((bf16[64,8,512]{2,1,0:T(8,128)(2,1)}), bf16[64,8,512]{2,1,0:T(8,128)(2,1)S(1)}, u32[]{:S(2)}, u32[]{:S(2)}) async-start(bf16[64,8,512]{2,1,0:T(8,128)(2,1)} %fusion.10), calls=%async_computation | async-start | bytes 1048576 | tf_op jit(solution)/shard_map/all_to_all | solution.py:46
  301.9 0.0 reduce-scatter.5.cloned.1.call-start
  302.0 0.7 compare_select_fusion.2
  302.7 1.4 scatter_custom_fusion
  304.1 0.7 compare_select_fusion.1
  304.8 0.0 copy-start.3
  304.8 1.9 gather_fusion
  306.7 0.7 compare_select_fusion.3
  307.4 1.0 fusion.42
  308.4 5.4 all-to-all-done
  313.8 0.8 gather_fusion.1
  314.6 0.0 all-gather.3.cloned.1.call-done
  314.6 5.7 bitcast_reduce_fusion
  320.3 0.1 multiply_convert_fusion.2
  320.4 0.7 gather_fusion.2
  321.1 0.0 all-gather.5.cloned.1.call-done
  321.1 3.4 bitcast_reduce_fusion.1
  324.5 0.2 fusion.29
  324.7 0.0 copy-done.3
  324.7 0.1 convert_reduce_fusion
  324.9 4.5 fusion.20
  329.4 0.0 reduce-scatter.5.cloned.1.call-update
  329.4 0.0 reduce-scatter.3.cloned.1.call-start
  329.5 4.4 convolution_bitcast_fusion.1
  333.9 0.0 copy-done.4
  333.9 0.4 convert_reduce_fusion.1
  334.3 0.1 broadcast_in_dim.27
  334.4 7.2 fusion.13
  341.6 0.0 reduce-scatter.3.cloned.1.call-update
  341.6 0.0 copy-start.1
  341.6 0.2 all-reduce.5.cloned.1.call-start
  341.8 6.7 convolution_bitcast_fusion
  348.6 0.8 fusion.2
  349.4 0.3 convert_element_type.127
  349.7 0.3 copy.41
  350.0 19.3 %all_to_all.26 = bf16[8,64,512]{2,0,1:T(8,128)(2,1)S(1)} all-to-all(bf16[8,64,512]{2,0,1:T(8,128)(2,1)S(1)} %copy.41), channel_id=1, replica_groups=mesh['table'=64,'rep'=4] {'table'}, dimensions={1} | all-to-all | bytes 1048576 | tf_op jit(solution)/shard_map/all_to_all | solution.py:98
  369.3 0.0 copy-done.1
  369.3 0.3 fusion.27
  369.7 270.1 %all-reduce.7 = bf16[512,256]{1,0:T(8,128)(2,1)S(1)} all-reduce(f32[512,256]{1,0:T(8,128)S(1)} %fusion.27), channel_id=1, replica_groups=mesh['table'=64,'rep'=4] {'table'}, use_global_device_ids=true, to_apply=%region_5.6 | all-reduce | flops 131072 | bytes 786432 | tf_op jit(solution)/shard_map/psum | solution.py:105
  639.8 1.0 fusion.3
  640.8 1.0 convolution_convert_fusion.1
  641.9 1.6 convert_element_type.143
  643.4 293.1 %reduce-scatter.3.cloned.1.call-done = f32[4,128,128]{2,1,0:T(8,128)} async-done(((f32[256,128,128]{2,1,0:T(8,128)}), f32[4,128,128]{2,1,0:T(8,128)}) %reduce-scatter.3.cloned.1.call-update) | async-done | bytes 262160 | tf_op jit(solution)/shard_map/reduce_scatter | solution.py:118
  936.5 1.6 convert_element_type.141
  938.2 0.0 all-reduce.5.cloned.1.call-update
  938.2 88.1 %psum.63 = f32[3,4096]{1,0:T(4,128)} all-reduce(f32[3,4096]{1,0:T(4,128)S(1)} %pad_maximum_fusion), channel_id=1, replica_groups=mesh['table'=64,'rep'=4] {'table','rep'}, use_global_device_ids=true, to_apply=%region_17.18 | all-reduce | flops 12288 | bytes 98304 | tf_op jit(solution)/shard_map/psum | solution.py:128
  1026.3 0.2 fusion.8
  1026.5 11.0 %psum.60 = bf16[512]{0:T(512)(128)(2,1)S(1)} all-reduce(bf16[512]{0:T(512)(128)(2,1)S(1)} %fusion.8), channel_id=1, replica_groups=mesh['table'=64,'rep'=4] {'rep'}, use_global_device_ids=true, to_apply=%region_9.10 | all-reduce | flops 512 | bytes 2048 | tf_op jit(solution)/shard_map/psum | solution.py:126
  1037.5 0.6 convert_element_type.140
  1038.1 2.1 fusion.1
  1040.1 1.5 convert_element_type.144
  1041.6 1.9 copy.42
  1043.5 1.6 convert_element_type.142
  1045.1 1.8 convert_element_type.138
  (16 shorter events, 0.2 us)
Async XLA Ops:
  7.2 276.1 %copy-start = (bf16[256,512]{1,0:T(8,128)(2,1)S(1)}, bf16[256,512]{1,0:T(8,128)(2,1)}, u32[]{:S(2)}) copy-start(bf16[256,512]{1,0:T(8,128)(2,1)} %param.15) | copy-start | bytes 786436
  7.2 307.4 %all-gather.3.cloned.1.call-start = ((), (), s32[]{:S(2)}) async-start(), calls=%async_computation.4 | async-start | bytes 8519680 | tf_op jit(solution)/shard_map/all_gather | solution.py:54
  7.9 313.2 %all-gather.5.cloned.1.call-start = ((), (), s32[]{:S(2)}) async-start(), calls=%async_computation.5 | async-start | bytes 4259840 | tf_op jit(solution)/shard_map/all_gather | solution.py:55
  286.3 27.5 %all-to-all-start = ((bf16[64,8,512]{2,1,0:T(8,128)(2,1)}), bf16[64,8,512]{2,1,0:T(8,128)(2,1)S(1)}, u32[]{:S(2)}, u32[]{:S(2)}) async-start(bf16[64,8,512]{2,1,0:T(8,128)(2,1)} %fusion.10), calls=%async_computation | async-start | bytes 1048576 | tf_op jit(solution)/shard_map/all_to_all | solution.py:46
  301.9 339.9 %reduce-scatter.5.cloned.1.call-start = ((), (), s32[]{:S(2)}) async-start(), calls=%async_computation.7 | async-start | bytes 8519680 | tf_op jit(solution)/shard_map/reduce_scatter | solution.py:119
  304.8 19.9 %copy-start.2 = (s32[1,8]{1,0:T(1,128)S(1)}, s32[1,8]{1,0:T(1,128)}, u32[]{:S(2)}) copy-start(s32[1,8]{1,0:T(1,128)} %param.22) | copy-start | bytes 100
  304.8 19.9 %copy-start.3 = (s32[1,8]{1,0:T(1,128)S(1)}, s32[1,8]{1,0:T(1,128)}, u32[]{:S(2)}) copy-start(s32[1,8]{1,0:T(1,128)} %param.23) | copy-start | bytes 100
  329.4 4.5 copy-start.4
  329.4 607.1 %reduce-scatter.3.cloned.1.call-start = ((), (), s32[]{:S(2)}) async-start(), calls=%async_computation.6 | async-start | bytes 17039360 | tf_op jit(solution)/shard_map/reduce_scatter | solution.py:118
  341.6 27.7 %copy-start.1 = (bf16[512,512]{1,0:T(8,128)(2,1)S(1)}, bf16[512,512]{1,0:T(8,128)(2,1)}, u32[]{:S(2)}) copy-start(bf16[512,512]{1,0:T(8,128)(2,1)} %param.12) | copy-start | bytes 1572868
  341.6 698.5 %all-reduce.5.cloned.1.call-start = ((), (), s32[]{:S(2)}) async-start(), calls=%async_computation.8 | async-start | bytes 1441792 | tf_op jit(solution)/shard_map/psum | solution.py:124
Sparse Core Ops, SparseCore 0:
  9.9 116.6 all-gather.2
  128.4 106.9 all-gather.4
  329.5 291.3 reduce-scatter.4
  623.4 313.0 reduce-scatter.2
  939.9 68.5 all-reduce.4
where the time goes:
time: 1050 us
  blocking collectives  662 us (63%)
  waiting for transfers between devices  300 us (29%)
  matrix products  39.9 us (4%)
  starting transfers between devices  16 us (2%)
  between operations  14 us (1%)
  other arithmetic  13.3 us (1%)
    reduce_scatter x1, waiting for transfers between devices, body(): lax.psum_scatter(local_one, 'table', scatter_dimension=0, tiled=True)  293 us
    psum x1, blocking collectives, body(): crossed = lax.psum(partial_sum, 'table').astype(jnp.bfloat16)  273 us
    psum x1, blocking collectives, body(): grad_crossed = lax.psum(partial_back, 'table').astype(jnp.bfloat16)  270 us
    psum x1, blocking collectives, body(): grad_vectors = lax.psum(vectors_local, ('table', 'rep'))  88.1 us
  transfers between devices with their start and end apart: 6, of which 2 were waited for; matrix products, arithmetic and copies ran while one was open for 4% of the time, Pallas kernels for 0%

commit v1 on v0

v1 whole, which is shorter than its diff:
```python
import jax
import jax.numpy as jnp
from jax import lax
from jax.sharding import PartitionSpec as P

E = 128
K1 = 8
K2 = 4
HB = 32
NT = 64
N_REP = 4
BF = jnp.bfloat16
F32 = jnp.float32


def silu_slope(value):
    squash = jax.nn.sigmoid(value)
    return squash * (1.0 + value * (1.0 - squash))


def exchange(parts):
    return lax.all_to_all(parts, "table", split_axis=0, concat_axis=0, tiled=True)


def from_rep(value, shift):
    return lax.ppermute(value, "rep", [(i, (i + shift) % N_REP) for i in range(N_REP)])


def rep_sum_scatter(quarters):
    mine = lax.axis_index("rep")
    total = lax.dynamic_index_in_dim(quarters, mine, 0, keepdims=False).astype(F32)
    for shift in (1, 2, 3):
        sent = lax.dynamic_index_in_dim(quarters, (mine + shift) % N_REP, 0, keepdims=False)
        total = total + from_rep(sent, shift).astype(F32)
    return total.astype(BF)


def rep_gather(quarter):
    mine = lax.axis_index("rep")
    whole = jnp.zeros((N_REP,) + quarter.shape, BF)
    whole = lax.dynamic_update_index_in_dim(whole, quarter, mine, 0)
    for shift in (1, 2, 3):
        whole = lax.dynamic_update_index_in_dim(
            whole, from_rep(quarter, shift), (mine - shift) % N_REP, 0
        )
    return whole


def split_pieces(blocks):
    return blocks.reshape(4, NT, 2, E).transpose(1, 0, 2, 3).reshape(NT, 8, E)


def join_pieces(pieces):
    return pieces.reshape(NT, 4, 2, E).transpose(1, 0, 2, 3).reshape(4, E, E)


def reorder(pieces, select):
    rows = pieces.reshape(NT * 4, 2 * E)
    moved = jnp.dot(select, rows, preferred_element_type=F32).astype(BF)
    return moved.reshape(NT, 8, E)


def body(
    pooled,
    table_slot,
    cross_v,
    cross_u,
    cross_bias,
    block_index1,
    weight1,
    block_index2,
    weight2,
    top_vectors,
    labels,
    importance,
):
    tables = table_slot.shape[0]
    contract_last = (((1,), (1,)), ((), ()))
    contract_first = (((0,), (0,)), ((), ()))
    full_two = lax.all_gather(weight2, "table", axis=0, tiled=True)

    reads = block_index1[:, None] == table_slot[None, :]
    reads_half = reads.astype(BF)
    hidden_of_slot = jnp.sum(
        jnp.where(reads, jnp.arange(tables, dtype=jnp.int32)[:, None] // K1, 0), axis=0
    )
    adds = (jnp.arange(HB, dtype=jnp.int32)[:, None] == hidden_of_slot[None, :]).astype(BF)

    partial = jnp.dot(pooled, cross_v, preferred_element_type=F32).astype(BF)
    got = exchange(
        jnp.concatenate([partial.reshape(NT, 8, 256), split_pieces(weight1)], axis=2)
    )
    crossed_own = jnp.sum(got[:, :, :256].astype(F32), axis=0).astype(BF)
    by_slot = reorder(got[:, :, 256:], reads_half.T)
    got = exchange(
        jnp.concatenate([jnp.broadcast_to(crossed_own[None], (NT, 8, 256)), by_slot], axis=2)
    )
    crossed = got[:, :, :256].reshape(512, 256)
    weight_slot = join_pieces(got[:, :, 256:])

    factor = jnp.dot(crossed, cross_u, preferred_element_type=F32) + cross_bias + 1.0
    lifted = (pooled.astype(F32) * factor).astype(BF)
    lifted_blocks = lifted.reshape(512, 4, E)
    terms = jnp.einsum("bqc,qcd->bqd", lifted_blocks, weight_slot, preferred_element_type=F32)
    got = exchange(terms.astype(BF).reshape(NT, 8, 512))
    terms_own = got.reshape(NT, 8, 4, E).transpose(0, 2, 1, 3).reshape(tables, 8 * E)
    preact_one = jnp.dot(adds, terms_own, preferred_element_type=F32).reshape(HB, 8, E)
    preact_one = preact_one.transpose(1, 0, 2) + top_vectors[0].reshape(-1, E)
    hidden_one = jax.nn.silu(preact_one).astype(BF)

    picked_two = hidden_one[:, block_index2]
    terms_two = jnp.einsum("bnc,ncd->bnd", picked_two, full_two, preferred_element_type=F32)
    preact_two = terms_two.reshape(8, HB, K2, E).sum(axis=2) + top_vectors[1].reshape(-1, E)
    hidden_two = jax.nn.silu(preact_two).astype(BF)
    last_weight = top_vectors[2].reshape(-1, E)
    logit = jnp.sum(hidden_two.astype(F32) * last_weight, axis=(1, 2))
    sample_weight = importance.reshape(-1).astype(F32) / 8.0
    targets = labels.reshape(-1).astype(F32)
    grad_logit = sample_weight * (jax.nn.sigmoid(logit) - targets)
    grad_two = (grad_logit[:, None, None] * last_weight * silu_slope(preact_two)).astype(BF)
    last_terms = (hidden_two.astype(F32) * grad_logit[:, None, None]).astype(BF)
    spread_two = jnp.repeat(grad_two, K2, axis=1)
    back_two = jnp.einsum("bnd,ncd->bnc", spread_two, full_two, preferred_element_type=F32)
    onehot_two = (block_index2[:, None] == jnp.arange(HB, dtype=jnp.int32)[None, :]).astype(F32)
    into_one = jnp.einsum("bnc,nj->bjc", back_two, onehot_two, precision=lax.Precision.HIGHEST)
    grad_one = (into_one * silu_slope(preact_one)).astype(BF)

    spread_one = grad_one[:, hidden_of_slot].reshape(8, NT, 4 * E)
    picked_pair = picked_two.reshape(8, NT, 2 * E)
    both = jnp.repeat(grad_two, 2, axis=1)
    third = jnp.stack([grad_one, last_terms], axis=2).reshape(8, NT, E)
    sent = jnp.concatenate([spread_one, picked_pair, both, third], axis=2).transpose(1, 0, 2)
    got = exchange(sent).reshape(512, 8 * E)
    grad_rows = got[:, : 4 * E]
    hidden_rows = got[:, 4 * E : 6 * E]
    two_rows = got[:, 6 * E : 7 * E]
    third_rows = got[:, 7 * E :]

    grad_rows_blocks = grad_rows.reshape(512, 4, E)
    back_one = jnp.einsum(
        "bqd,qcd->bqc", grad_rows_blocks, weight_slot, preferred_element_type=F32
    )
    grad_lifted = back_one.astype(BF).reshape(512, 512)
    local_one = jnp.einsum(
        "bqc,bqd->qcd", lifted_blocks, grad_rows_blocks, preferred_element_type=F32
    )
    local_two = lax.dot_general(
        hidden_rows, two_rows, contract_first, preferred_element_type=F32
    )
    vector_rows = jnp.stack(
        [jnp.sum(two_rows.astype(F32), axis=0), jnp.sum(third_rows.astype(F32), axis=0)]
    )
    vector_sum = (vector_rows + from_rep(vector_rows, 2)) + (
        from_rep(vector_rows, 1) + from_rep(vector_rows, 3)
    )

    cross_grad = grad_lifted.astype(F32) * pooled.astype(F32)
    cross_half = cross_grad.astype(BF)
    direct = grad_lifted.astype(F32) * factor
    partial_back = lax.dot_general(
        cross_half, cross_u, contract_last, preferred_element_type=F32
    ).astype(BF)
    got = exchange(
        jnp.concatenate(
            [partial_back.reshape(NT, 8, 256), split_pieces(local_one.astype(BF))], axis=2
        )
    )
    back_own = jnp.sum(got[:, :, :256].astype(F32), axis=0).astype(BF)
    by_block = reorder(got[:, :, 256:], reads_half)
    shared = jnp.concatenate(
        [back_own, jnp.pad(vector_sum.astype(BF), ((0, 6), (0, 0)))], axis=1
    )

    local_u = lax.dot_general(crossed, cross_half, contract_first, preferred_element_type=F32)
    local_bias = jnp.sum(cross_grad, axis=0)
    early = jnp.concatenate(
        [
            local_u.astype(BF).reshape(N_REP, 64, 512),
            local_two.astype(BF).reshape(N_REP, 16, 512),
            jnp.pad(local_bias.astype(BF).reshape(N_REP, 1, 128), ((0, 0), (0, 7), (0, 384))),
        ],
        axis=1,
    )
    early_quarter = rep_sum_scatter(early)

    got = exchange(
        jnp.concatenate([jnp.broadcast_to(shared[None], (NT, 8, 384)), by_block], axis=2)
    )
    grad_crossed = got[:, :, :256].reshape(512, 256)
    vectors = got[:, :2, 256:384].astype(F32)
    summed_one = join_pieces(got[:, :, 384:])
    early_whole = rep_gather(early_quarter)

    local_v = lax.dot_general(pooled, grad_crossed, contract_first, preferred_element_type=F32)
    late = jnp.concatenate(
        [
            local_v.astype(BF).reshape(N_REP, 128, 256),
            summed_one.reshape(N_REP, 64, 256),
        ],
        axis=1,
    )
    late_whole = rep_gather(rep_sum_scatter(late))
    d_pooled = (
        direct + lax.dot_general(grad_crossed, cross_v, contract_last, preferred_element_type=F32)
    ).astype(BF)

    grad_u = early_whole[:, :64].reshape(256, 512).astype(F32)
    grad_w2 = early_whole[:, 64:80].reshape(2, E, E).astype(F32)
    grad_bias = early_whole[:, 80, :128].reshape(512).astype(F32)
    grad_v = late_whole[:, :128].reshape(512, 256).astype(F32)
    grad_w1 = late_whole[:, 128:].reshape(4, E, E).astype(F32)
    pairs = vectors.reshape(HB, 2, 2, E)
    grad_vectors = jnp.stack(
        [pairs[:, 0, 1].reshape(-1), pairs[:, 0, 0].reshape(-1), pairs[:, 1, 1].reshape(-1)]
    )
    return (d_pooled, grad_v, grad_u, grad_bias, grad_w1, grad_w2, grad_vectors)


def solution(mesh):
    placed = (
        P("rep", "table"),
        P(),
        P("table", None),
        P(None, "table"),
        P("table"),
        P(),
        P("table", None, None),
        P(),
        P("table", None, None),
        P(),
        P("rep", "table"),
        P("rep", "table"),
    )
    return jax.shard_map(
        body,
        mesh=mesh,
        in_specs=placed,
        out_specs=(
            P("rep", "table"),
            P("table", None),
            P(None, "table"),
            P("table"),
            P("table", None, None),
            P("table", None, None),
            P(),
        ),
        check_vma=False,
    )
```

time: 1050 us -> 264 us (0.25)
  blocking collectives: 662 us -> 19.6 us
  waiting for transfers between devices: 300 us -> 123 us
  starting transfers between devices: 16 us -> 68 us
  matrix products: 39.9 us -> 13.8 us
    psum x4 -> x0, blocking collectives: 642 us -> none  [the longest x1 273 us: body(): crossed = lax.psum(partial_sum, 'table').astype(jnp.bfloat16)]
    reduce_scatter x2 -> x0, waiting for transfers between devices: 293 us -> none  [the longest x1 293 us: body(): lax.psum_scatter(local_one, 'table', scatter_dimension=0, tiled=True)]
    all_gather x2 -> x1, waiting for transfers between devices: 0.04 us -> 53.5 us  [body(): full_two = lax.all_gather(weight2, 'table', axis=0, tiled=True)]
    all_to_all x1 -> x5, waiting for transfers between devices: 5.35 us -> 48.4 us  [exchange(): lax.all_to_all(parts, 'table', split_axis=0, concat_axis=0, tiled=True)]
    ppermute x0 -> x15, starting transfers between devices: none -> 33.6 us  [from_rep(): lax.ppermute(value, 'rep', [(i, (i + shift) % N_REP) for i in range(N_REP)])]
    dot_general x9 -> x11, matrix products: 35.1 us -> 12.1 us  [the longest x1 3.53 us: body(): jnp.einsum('bnc,ncd->bnd', picked_two, full_two, preferred_element_type=F32)]
    ppermute x0 -> x15, waiting for transfers between devices: none -> 20 us  [from_rep(): lax.ppermute(value, 'rep', [(i, (i + shift) % N_REP) for i in range(N_REP)])]
    all_to_all x1 -> x5, starting transfers between devices: 15.7 us -> 34.4 us  [exchange(): lax.all_to_all(parts, 'table', split_axis=0, concat_axis=0, tiled=True)]
  transfers between devices with their start and end apart: 6 -> 21, of which waited for: 2 -> 12; matrix products, arithmetic and copies ran while one was open for 4% -> 7% of each run, Pallas kernels for 0% -> 0%
where the time goes in v1:
time: 264 us; the launch traced here: 263 us
  waiting for transfers between devices  123 us (47%)
  starting transfers between devices  68 us (26%)
  blocking collectives  19.6 us (7%)
  between operations  14.9 us (6%)
  local copies, waits for them, and re-layouts  14 us (5%)
  matrix products  13.8 us (5%)
  other arithmetic  9.8 us (4%)
    all_gather x1, waiting for transfers between devices, body(): full_two = lax.all_gather(weight2, 'table', axis=0, tiled=True)  53.5 us
    all_to_all x5, waiting for transfers between devices, exchange(): lax.all_to_all(parts, 'table', split_axis=0, concat_axis=0, tiled=True)  48.4 us
    all_to_all x5, starting transfers between devices, exchange(): lax.all_to_all(parts, 'table', split_axis=0, concat_axis=0, tiled=True)  34.4 us
    ppermute x15, starting transfers between devices, from_rep(): lax.ppermute(value, 'rep', [(i, (i + shift) % N_REP) for i in range(N_REP)])  33.6 us
    ppermute x15, waiting for transfers between devices, from_rep(): lax.ppermute(value, 'rep', [(i, (i + shift) % N_REP) for i in range(N_REP)])  20 us
    all_to_all x1, blocking collectives, exchange(): lax.all_to_all(parts, 'table', split_axis=0, concat_axis=0, tiled=True)  19.6 us
  transfers between devices with their start and end apart: 21, of which 12 were waited for; matrix products, arithmetic and copies ran while one was open for 7% of the time, Pallas kernels for 0%

profile of v1, /device:TPU:2, one launch (start us, length us, event | category | flops | bytes accessed | tf_op | source)
XLA Modules:
  0.0 262.6 jit_solution(12785818179895529104)
XLA Ops:
  7.3 0.7 all-gather.2.cloned.1.call-update
  8.0 1.0 copy.186
  9.0 1.4 fusion.4
  10.4 19.6 %all_to_all.30 = bf16[64,8,384]{2,1,0:T(8,128)(2,1)S(1)} all-to-all(bf16[64,8,384]{2,1,0:T(8,128)(2,1)S(1)} %pad_maximum_fusion.1), channel_id=1, replica_groups=mesh['table'=64,'rep'=4] {'table'}, dimensions={0} | all-to-all | bytes 786432 | tf_op jit(solution)/shard_map/all_to_all | solution.py:22
  30.1 1.0 convolution_convert_fusion.8
  31.2 0.8 pad_maximum_fusion.2
  32.0 5.6 %all-to-all-start.1 = ((bf16[64,8,384]{2,1,0:T(8,128)(2,1)}), bf16[64,8,384]{2,1,0:T(8,128)(2,1)S(1)}, u32[]{:S(2)}, u32[]{:S(2)}) async-start(bf16[64,8,384]{2,1,0:T(8,128)(2,1)} %pad_maximum_fusion.2), calls=%async_computation.1 | async-start | bytes 786432 | tf_op jit(solution)/shard_map/all_to_all | solution.py:22
  38.0 10.0 %all-to-all-done.1 = bf16[64,8,384]{2,1,0:T(8,128)(2,1)S(1)} async-done(((bf16[64,8,384]{2,1,0:T(8,128)(2,1)}), bf16[64,8,384]{2,1,0:T(8,128)(2,1)S(1)}, u32[]{:S(2)}, u32[]{:S(2)}) %all-to-all-start.1) | async-done | bytes 393248 | tf_op jit(solution)/shard_map/all_to_all | solution.py:22
  48.3 0.4 fusion.10
  48.7 1.1 fusion.3
  49.8 1.4 copy.192
  51.2 1.0 reshape.273
  52.2 6.2 %all-to-all-start.2 = ((bf16[64,8,512]{2,1,0:T(8,128)(2,1)}), bf16[64,8,512]{2,1,0:T(8,128)(2,1)S(1)}, u32[]{:S(2)}, u32[]{:S(2)}) async-start(bf16[64,8,512]{2,1,0:T(8,128)(2,1)} %reshape.273), calls=%async_computation.2 | async-start | bytes 1048576 | tf_op jit(solution)/shard_map/all_to_all | solution.py:22
  58.4 11.7 %all-to-all-done.2 = bf16[64,8,512]{2,1,0:T(8,128)(2,1)S(1)} async-done(((bf16[64,8,512]{2,1,0:T(8,128)(2,1)}), bf16[64,8,512]{2,1,0:T(8,128)(2,1)S(1)}, u32[]{:S(2)}, u32[]{:S(2)}) %all-to-all-start.2) | async-done | bytes 524320 | tf_op jit(solution)/shard_map/all_to_all | solution.py:22
  70.1 0.9 copy.239
  71.0 1.2 copy.193
  72.6 0.7 gather_fusion
  73.3 53.5 %all-gather.2.cloned.1.call-done = bf16[128,128,128]{2,1,0:T(8,128)(2,1)} async-done(((bf16[2,128,128]{2,1,0:T(8,128)(2,1)}), bf16[128,128,128]{2,1,0:T(8,128)(2,1)}) %all-gather.2.cloned.1.call-update) | async-done | bytes 4194320 | tf_op jit(solution)/shard_map/all_gather | solution.py:80
  126.7 3.5 %bitcast_reduce_fusion = f32[8,32,128]{2,0,1:T(8,128)S(1)} fusion(bf16[128,128,128]{2,1,0:T(8,128)(2,1)} %all-gather.2.cloned.1.call-done, bf16[128,8,128]{2,1,0:T(8,128)(2,1)S(1)} %gather_fusion), kind=kOutput, calls=%fused_computation.42 | convolution fusion | flops 33652736 | bytes 4587520 | tf_op jit(solution)/shard_map/bnc,ncd->bnd/dot_general | solution.py:112
  130.7 2.3 convolution_bitcast_fusion
  133.0 0.4 fusion.9
  133.5 0.8 gather_fusion.1
  134.3 1.1 maximum_bitcast_fusion
  135.5 6.8 %all-to-all-start.3 = ((bf16[64,8,1024]{2,1,0:T(8,128)(2,1)}), bf16[64,8,1024]{2,1,0:T(8,128)(2,1)S(1)}, u32[]{:S(2)}, u32[]{:S(2)}) async-start(bf16[64,8,1024]{2,1,0:T(8,128)(2,1)} %maximum_bitcast_fusion), calls=%async_computation.3 | async-start | bytes 2097152 | tf_op jit(solution)/shard_map/all_to_all | solution.py:22
  142.4 17.2 %all-to-all-done.3 = bf16[64,8,1024]{2,1,0:T(8,128)(2,1)S(1)} async-done(((bf16[64,8,1024]{2,1,0:T(8,128)(2,1)}), bf16[64,8,1024]{2,1,0:T(8,128)(2,1)S(1)}, u32[]{:S(2)}, u32[]{:S(2)}) %all-to-all-start.3) | async-done | bytes 1048608 | tf_op jit(solution)/shard_map/all_to_all | solution.py:22
  159.6 1.0 copy-done.3
  160.6 0.8 slice.104
  161.4 1.3 copy.202
  163.3 1.1 convert_reduce_fusion.1
  164.4 1.3 convolution_convert_fusion.9
  165.7 1.2 fusion.11
  167.3 0.8 pad_maximum_fusion.3
  168.0 5.7 %all-to-all-start.4 = ((bf16[64,8,384]{2,1,0:T(8,128)(2,1)}), bf16[64,8,384]{2,1,0:T(8,128)(2,1)S(1)}, u32[]{:S(2)}, u32[]{:S(2)}) async-start(bf16[64,8,384]{2,1,0:T(8,128)(2,1)} %pad_maximum_fusion.3), calls=%async_computation.4 | async-start | bytes 786432 | tf_op jit(solution)/shard_map/all_to_all | solution.py:22
  174.2 4.5 %collective-permute-start.11 = (bf16[88,512]{1,0:T(8,128)(2,1)S(1)}, bf16[88,512]{1,0:T(8,128)(2,1)S(1)}, u32[]{:S(2)}, u32[]{:S(2)}) collective-permute-start(bf16[88,512]{1,0:T(8,128)(2,1)S(1)} %get-tuple-element.76), channel_id=1, source_target_pairs={{0,3},{1,0},{2,1},{3,2},{4,7},{5,4},{6,5},{7,6},{8,11},{9,8},{10,9... | collective-permute-start | bytes 270344 | tf_op jit(solution)/shard_map/ppermute | solution.py:26
  178.8 2.9 %collective-permute-start.10 = (bf16[88,512]{1,0:T(8,128)(2,1)S(1)}, bf16[88,512]{1,0:T(8,128)(2,1)S(1)}, u32[]{:S(2)}, u32[]{:S(2)}) collective-permute-start(bf16[88,512]{1,0:T(8,128)(2,1)S(1)} %get-tuple-element.77), channel_id=1, source_target_pairs={{0,2},{1,3},{2,0},{3,1},{4,6},{5,7},{6,4},{7,5},{8,10},{9,11},{10,... | collective-permute-start | bytes 270344 | tf_op jit(solution)/shard_map/ppermute | solution.py:26
  181.7 1.2 collective-permute-start.9
  182.9 2.4 collective-permute-start.1
  185.3 1.7 collective-permute-start.2
  187.0 1.9 collective-permute-start
  188.9 1.1 collective-permute-done.10
  190.2 1.1 collective-permute-start.12
  191.3 3.2 %collective-permute-done = f32[2,128]{1,0:T(2,128)S(1)} collective-permute-done((f32[2,128]{1,0:T(2,128)S(1)}, f32[2,128]{1,0:T(2,128)S(1)}, u32[]{:S(2)}, u32[]{:S(2)}) %collective-permute-start) | collective-permute-done | bytes 1056 | tf_op jit(solution)/shard_map/ppermute | solution.py:26
  194.5 2.1 collective-permute-start.13
  196.6 2.8 %collective-permute-start.14 = (bf16[88,512]{1,0:T(8,128)(2,1)S(1)}, bf16[88,512]{1,0:T(8,128)(2,1)S(1)}, u32[]{:S(2)}, u32[]{:S(2)}) collective-permute-start(bf16[88,512]{1,0:T(8,128)(2,1)S(1)} %get-tuple-element.66), channel_id=1, source_target_pairs={{0,3},{1,0},{2,1},{3,2},{4,7},{5,4},{6,5},{7,6},{8,11},{9,8},{10,9... | collective-permute-start | bytes 270344 | tf_op jit(solution)/shard_map/ppermute | solution.py:26
  199.9 0.8 pad_maximum_fusion
  200.7 10.1 %all-to-all-start.5 = ((bf16[64,8,512]{2,1,0:T(8,128)(2,1)}), bf16[64,8,512]{2,1,0:T(8,128)(2,1)S(1)}, u32[]{:S(2)}, u32[]{:S(2)}) async-start(bf16[64,8,512]{2,1,0:T(8,128)(2,1)} %pad_maximum_fusion), calls=%async_computation.5 | async-start | bytes 1048576 | tf_op jit(solution)/shard_map/all_to_all | solution.py:22
  211.0 0.7 reshape.303
  211.7 0.6 slice_convert_fusion.2
  212.2 0.9 bitcast_convert_fusion
  213.1 9.5 %all-to-all-done.5 = bf16[64,8,512]{2,1,0:T(8,128)(2,1)S(1)} async-done(((bf16[64,8,512]{2,1,0:T(8,128)(2,1)}), bf16[64,8,512]{2,1,0:T(8,128)(2,1)S(1)}, u32[]{:S(2)}, u32[]{:S(2)}) %all-to-all-start.5) | async-done | bytes 524320 | tf_op jit(solution)/shard_map/all_to_all | solution.py:22
  223.2 0.7 collective-permute-start.5
  223.9 4.9 %collective-permute-start.4 = (bf16[192,256]{1,0:T(8,128)(2,1)S(1)}, bf16[192,256]{1,0:T(8,128)(2,1)S(1)}, u32[]{:S(2)}, u32[]{:S(2)}) collective-permute-start(bf16[192,256]{1,0:T(8,128)(2,1)S(1)} %get-tuple-element.73), channel_id=1, source_target_pairs={{0,2},{1,3},{2,0},{3,1},{4,6},{5,7},{6,4},{7,5},{8,10},{9,11},{10,... | collective-permute-start | bytes 294920 | tf_op jit(solution)/shard_map/ppermute | solution.py:26
  228.9 0.7 pad_maximum_fusion.5
  229.6 2.9 %collective-permute-done.5 = bf16[192,256]{1,0:T(8,128)(2,1)S(1)} collective-permute-done((bf16[192,256]{1,0:T(8,128)(2,1)S(1)}, bf16[192,256]{1,0:T(8,128)(2,1)S(1)}, u32[]{:S(2)}, u32[]{:S(2)}) %collective-permute-start.5) | collective-permute-done | bytes 98336 | tf_op jit(solution)/shard_map/ppermute | solution.py:26
  232.5 3.8 %collective-permute-done.4 = bf16[192,256]{1,0:T(8,128)(2,1)S(1)} collective-permute-done((bf16[192,256]{1,0:T(8,128)(2,1)S(1)}, bf16[192,256]{1,0:T(8,128)(2,1)S(1)}, u32[]{:S(2)}, u32[]{:S(2)}) %collective-permute-start.4) | collective-permute-done | bytes 98336 | tf_op jit(solution)/shard_map/ppermute | solution.py:26
  236.3 1.5 collective-permute-done.3
  237.9 1.3 collective-permute-start.6
  239.5 1.0 copy.212
  240.5 2.5 collective-permute-start.7
  243.0 3.6 %collective-permute-start.8 = (bf16[192,256]{1,0:T(8,128)(2,1)S(1)}, bf16[192,256]{1,0:T(8,128)(2,1)S(1)}, u32[]{:S(2)}, u32[]{:S(2)}) collective-permute-start(bf16[192,256]{1,0:T(8,128)(2,1)S(1)} %get-tuple-element.68), channel_id=1, source_target_pairs={{0,3},{1,0},{2,1},{3,2},{4,7},{5,4},{6,5},{7,6},{8,11},{9,8},{10,9... | collective-permute-start | bytes 294920 | tf_op jit(solution)/shard_map/ppermute | solution.py:26
  246.6 2.5 collective-permute-done.7
  249.1 5.0 %collective-permute-done.8 = bf16[192,256]{1,0:T(8,128)(2,1)S(1)} collective-permute-done((bf16[192,256]{1,0:T(8,128)(2,1)S(1)}, bf16[192,256]{1,0:T(8,128)(2,1)S(1)}, u32[]{:S(2)}, u32[]{:S(2)}) %collective-permute-start.8) | collective-permute-done | bytes 98336 | tf_op jit(solution)/shard_map/ppermute | solution.py:26
  254.2 0.8 bitcast_convert_fusion.1
  255.1 0.7 reshape.302
  (114 shorter events, 5.0 us)
Async XLA Ops:
  7.2 41.1 %copy-start = (bf16[256,512]{1,0:T(8,128)(2,1)S(1)}, bf16[256,512]{1,0:T(8,128)(2,1)}, u32[]{:S(2)}) copy-start(bf16[256,512]{1,0:T(8,128)(2,1)} %param.15) | copy-start | bytes 786436
  7.2 30.4 %copy-start.6 = (bf16[512,512]{1,0:T(8,128)(2,1)S(1)}, bf16[512,512]{1,0:T(8,128)(2,1)}, u32[]{:S(2)}) copy-start(bf16[512,512]{1,0:T(8,128)(2,1)} %param.12) | copy-start | bytes 1572868
  7.2 30.7 %copy-start.10 = (s32[256]{0:T(256)S(1)}, s32[256]{0:T(256)}, u32[]{:S(2)}) copy-start(s32[256]{0:T(256)} %param.13) | copy-start | bytes 3076
  7.2 30.7 %copy-start.11 = (s32[256]{0:T(256)S(1)}, s32[256]{0:T(256)}, u32[]{:S(2)}) copy-start(s32[256]{0:T(256)} %param.17) | copy-start | bytes 3076
  7.2 30.8 %copy-start.15 = (s32[128]{0:T(128)S(1)}, s32[128]{0:T(128)}, u32[]{:S(2)}) copy-start(s32[128]{0:T(128)} %param.19) | copy-start | bytes 1540
  7.2 41.0 %copy-start.12 = (f32[512]{0:T(512)S(1)}, f32[512]{0:T(512)}, u32[]{:S(2)}) copy-start(f32[512]{0:T(512)} %param.16) | copy-start | bytes 6148
  7.2 119.5 %all-gather.2.cloned.1.call-start = ((), (), s32[]{:S(2)}) async-start(), calls=%async_computation.6 | async-start | bytes 4259840 | tf_op jit(solution)/shard_map/all_gather | solution.py:80
  32.0 16.0 %all-to-all-start.1 = ((bf16[64,8,384]{2,1,0:T(8,128)(2,1)}), bf16[64,8,384]{2,1,0:T(8,128)(2,1)S(1)}, u32[]{:S(2)}, u32[]{:S(2)}) async-start(bf16[64,8,384]{2,1,0:T(8,128)(2,1)} %pad_maximum_fusion.2), calls=%async_computation.1 | async-start | bytes 786432 | tf_op jit(solution)/shard_map/all_to_all | solution.py:22
  37.6 20.7 %copy-start.9 = (f32[3,4096]{1,0:T(4,128)S(1)}, f32[3,4096]{1,0:T(4,128)}, u32[]{:S(2)}) copy-start(f32[3,4096]{1,0:T(4,128)} %param.21) | copy-start | bytes 147460
  48.1 22.9 %copy-start.4 = (bf16[64,8,384]{2,1,0:T(8,128)(2,1)}, bf16[64,8,384]{2,1,0:T(8,128)(2,1)S(1)}, u32[]{:S(2)}) copy-start(bf16[64,8,384]{2,1,0:T(8,128)(2,1)S(1)} %all-to-all-done.1) | copy-start | bytes 1179652
  52.2 17.9 %all-to-all-start.2 = ((bf16[64,8,512]{2,1,0:T(8,128)(2,1)}), bf16[64,8,512]{2,1,0:T(8,128)(2,1)S(1)}, u32[]{:S(2)}, u32[]{:S(2)}) async-start(bf16[64,8,512]{2,1,0:T(8,128)(2,1)} %reshape.273), calls=%async_computation.2 | async-start | bytes 1048576 | tf_op jit(solution)/shard_map/all_to_all | solution.py:22
  70.1 60.3 %copy-start.13 = (s32[1,8]{1,0:T(1,128)S(1)}, s32[1,8]{1,0:T(1,128)}, u32[]{:S(2)}) copy-start(s32[1,8]{1,0:T(1,128)} %param.22) | copy-start | bytes 100
  70.1 60.3 %copy-start.14 = (s32[1,8]{1,0:T(1,128)S(1)}, s32[1,8]{1,0:T(1,128)}, u32[]{:S(2)}) copy-start(s32[1,8]{1,0:T(1,128)} %param.23) | copy-start | bytes 100
  126.7 4.0 %copy-start.1 = (bf16[128,128,128]{2,1,0:T(8,128)(2,1)S(1)}, bf16[128,128,128]{2,1,0:T(8,128)(2,1)}, u32[]{:S(2)}) copy-start(bf16[128,128,128]{2,1,0:T(8,128)(2,1)} %all-gather.2.cloned.1.call-done) | copy-start | bytes 12582916
  135.5 24.1 %all-to-all-start.3 = ((bf16[64,8,1024]{2,1,0:T(8,128)(2,1)}), bf16[64,8,1024]{2,1,0:T(8,128)(2,1)S(1)}, u32[]{:S(2)}, u32[]{:S(2)}) async-start(bf16[64,8,1024]{2,1,0:T(8,128)(2,1)} %maximum_bitcast_fusion), calls=%async_computation.3 | async-start | bytes 2097152 | tf_op jit(solution)/shard_map/all_to_all | solution.py:22
  159.6 1.0 copy-start.3
  163.2 10.6 %copy-start.5 = (bf16[64,8,384]{2,1,0:T(8,128)(2,1)S(1)}, bf16[64,8,384]{2,1,0:T(8,128)(2,1)}, u32[]{:S(2)}) copy-start(bf16[64,8,384]{2,1,0:T(8,128)(2,1)} %copy-done.4) | copy-start | bytes 1179652
  168.0 31.3 %all-to-all-start.4 = ((bf16[64,8,384]{2,1,0:T(8,128)(2,1)}), bf16[64,8,384]{2,1,0:T(8,128)(2,1)S(1)}, u32[]{:S(2)}, u32[]{:S(2)}) async-start(bf16[64,8,384]{2,1,0:T(8,128)(2,1)} %pad_maximum_fusion.3), calls=%async_computation.4 | async-start | bytes 786432 | tf_op jit(solution)/shard_map/all_to_all | solution.py:22
  174.2 48.5 %copy-start.7 = (bf16[512,512]{1,0:T(8,128)(2,1)S(1)}, bf16[512,512]{1,0:T(8,128)(2,1)}, u32[]{:S(2)}) copy-start(bf16[512,512]{1,0:T(8,128)(2,1)} %param.12) | copy-start | bytes 1572868
  174.2 12.8 %collective-permute-start.11 = (bf16[88,512]{1,0:T(8,128)(2,1)S(1)}, bf16[88,512]{1,0:T(8,128)(2,1)S(1)}, u32[]{:S(2)}, u32[]{:S(2)}) collective-permute-start(bf16[88,512]{1,0:T(8,128)(2,1)S(1)} %get-tuple-element.76), channel_id=1, source_target_pairs={{0,3},{1,0},{2,1},{3,2},{4,7},{5,4},{6,5},{7,6},{8,11},{9,8},{10,9... | collective-permute-start | bytes 270344 | tf_op jit(solution)/shard_map/ppermute | solution.py:26
  178.8 11.3 %collective-permute-start.10 = (bf16[88,512]{1,0:T(8,128)(2,1)S(1)}, bf16[88,512]{1,0:T(8,128)(2,1)S(1)}, u32[]{:S(2)}, u32[]{:S(2)}) collective-permute-start(bf16[88,512]{1,0:T(8,128)(2,1)S(1)} %get-tuple-element.77), channel_id=1, source_target_pairs={{0,2},{1,3},{2,0},{3,1},{4,6},{5,7},{6,4},{7,5},{8,10},{9,11},{10,... | collective-permute-start | bytes 270344 | tf_op jit(solution)/shard_map/ppermute | solution.py:26
  181.7 8.4 %collective-permute-start.9 = (bf16[88,512]{1,0:T(8,128)(2,1)S(1)}, bf16[88,512]{1,0:T(8,128)(2,1)S(1)}, u32[]{:S(2)}, u32[]{:S(2)}) collective-permute-start(bf16[88,512]{1,0:T(8,128)(2,1)S(1)} %get-tuple-element.75), channel_id=1, source_target_pairs={{0,1},{1,2},{2,3},{3,0},{4,5},{5,6},{6,7},{7,4},{8,9},{9,10},{10,1... | collective-permute-start | bytes 270344 | tf_op jit(solution)/shard_map/ppermute | solution.py:26
  182.9 8.4 %collective-permute-start.1 = (f32[2,128]{1,0:T(2,128)S(1)}, f32[2,128]{1,0:T(2,128)S(1)}, u32[]{:S(2)}, u32[]{:S(2)}) collective-permute-start(f32[2,128]{1,0:T(2,128)S(1)} %pad_maximum_fusion.6), channel_id=1, source_target_pairs={{0,1},{1,2},{2,3},{3,0},{4,5},{5,6},{6,7},{7,4},{8,9},{9,10},{10,1... | collective-permute-start | bytes 3080 | tf_op jit(solution)/shard_map/ppermute | solution.py:26
  185.3 6.0 %collective-permute-start.2 = (f32[2,128]{1,0:T(2,128)S(1)}, f32[2,128]{1,0:T(2,128)S(1)}, u32[]{:S(2)}, u32[]{:S(2)}) collective-permute-start(f32[2,128]{1,0:T(2,128)S(1)} %pad_maximum_fusion.6), channel_id=1, source_target_pairs={{0,3},{1,0},{2,1},{3,2},{4,7},{5,4},{6,5},{7,6},{8,11},{9,8},{10,9... | collective-permute-start | bytes 3080 | tf_op jit(solution)/shard_map/ppermute | solution.py:26
  187.0 7.5 %collective-permute-start = (f32[2,128]{1,0:T(2,128)S(1)}, f32[2,128]{1,0:T(2,128)S(1)}, u32[]{:S(2)}, u32[]{:S(2)}) collective-permute-start(f32[2,128]{1,0:T(2,128)S(1)} %pad_maximum_fusion.6), channel_id=1, source_target_pairs={{0,2},{1,3},{2,0},{3,1},{4,6},{5,7},{6,4},{7,5},{8,10},{9,11},{10,... | collective-permute-start | bytes 3080 | tf_op jit(solution)/shard_map/ppermute | solution.py:26
  190.2 9.2 %collective-permute-start.12 = (bf16[88,512]{1,0:T(8,128)(2,1)S(1)}, bf16[88,512]{1,0:T(8,128)(2,1)S(1)}, u32[]{:S(2)}, u32[]{:S(2)}) collective-permute-start(bf16[88,512]{1,0:T(8,128)(2,1)S(1)} %get-tuple-element.66), channel_id=1, source_target_pairs={{0,1},{1,2},{2,3},{3,0},{4,5},{5,6},{6,7},{7,4},{8,9},{9,10},{10,1... | collective-permute-start | bytes 270344 | tf_op jit(solution)/shard_map/ppermute | solution.py:26
  194.5 16.4 %collective-permute-start.13 = (bf16[88,512]{1,0:T(8,128)(2,1)S(1)}, bf16[88,512]{1,0:T(8,128)(2,1)S(1)}, u32[]{:S(2)}, u32[]{:S(2)}) collective-permute-start(bf16[88,512]{1,0:T(8,128)(2,1)S(1)} %get-tuple-element.66), channel_id=1, source_target_pairs={{0,2},{1,3},{2,0},{3,1},{4,6},{5,7},{6,4},{7,5},{8,10},{9,11},{10,... | collective-permute-start | bytes 270344 | tf_op jit(solution)/shard_map/ppermute | solution.py:26
  196.6 14.4 %collective-permute-start.14 = (bf16[88,512]{1,0:T(8,128)(2,1)S(1)}, bf16[88,512]{1,0:T(8,128)(2,1)S(1)}, u32[]{:S(2)}, u32[]{:S(2)}) collective-permute-start(bf16[88,512]{1,0:T(8,128)(2,1)S(1)} %get-tuple-element.66), channel_id=1, source_target_pairs={{0,3},{1,0},{2,1},{3,2},{4,7},{5,4},{6,5},{7,6},{8,11},{9,8},{10,9... | collective-permute-start | bytes 270344 | tf_op jit(solution)/shard_map/ppermute | solution.py:26
  200.7 38.4 %copy-start.2 = (f32[512,512]{0,1:T(8,128)S(1)}, f32[512,512]{0,1:T(8,128)}, u32[]{:S(2)}) copy-start(f32[512,512]{0,1:T(8,128)} %get-tuple-element.71) | copy-start | bytes 3145732
  200.7 38.4 %copy-start.8 = (bf16[512,256]{1,0:T(8,128)(2,1)S(1)}, bf16[512,256]{1,0:T(8,128)(2,1)}, u32[]{:S(2)}) copy-start(bf16[512,256]{1,0:T(8,128)(2,1)} %param.14) | copy-start | bytes 786436
  200.7 21.9 %all-to-all-start.5 = ((bf16[64,8,512]{2,1,0:T(8,128)(2,1)}), bf16[64,8,512]{2,1,0:T(8,128)(2,1)S(1)}, u32[]{:S(2)}, u32[]{:S(2)}) async-start(bf16[64,8,512]{2,1,0:T(8,128)(2,1)} %pad_maximum_fusion), calls=%async_computation.5 | async-start | bytes 1048576 | tf_op jit(solution)/shard_map/all_to_all | solution.py:22
  223.2 9.2 %collective-permute-start.5 = (bf16[192,256]{1,0:T(8,128)(2,1)S(1)}, bf16[192,256]{1,0:T(8,128)(2,1)S(1)}, u32[]{:S(2)}, u32[]{:S(2)}) collective-permute-start(bf16[192,256]{1,0:T(8,128)(2,1)S(1)} %get-tuple-element.74), channel_id=1, source_target_pairs={{0,3},{1,0},{2,1},{3,2},{4,7},{5,4},{6,5},{7,6},{8,11},{9,8},{10,9... | collective-permute-start | bytes 294920 | tf_op jit(solution)/shard_map/ppermute | solution.py:26
  223.9 12.4 %collective-permute-start.4 = (bf16[192,256]{1,0:T(8,128)(2,1)S(1)}, bf16[192,256]{1,0:T(8,128)(2,1)S(1)}, u32[]{:S(2)}, u32[]{:S(2)}) collective-permute-start(bf16[192,256]{1,0:T(8,128)(2,1)S(1)} %get-tuple-element.73), channel_id=1, source_target_pairs={{0,2},{1,3},{2,0},{3,1},{4,6},{5,7},{6,4},{7,5},{8,10},{9,11},{10,... | collective-permute-start | bytes 294920 | tf_op jit(solution)/shard_map/ppermute | solution.py:26
  228.8 9.0 %collective-permute-start.3 = (bf16[192,256]{1,0:T(8,128)(2,1)S(1)}, bf16[192,256]{1,0:T(8,128)(2,1)S(1)}, u32[]{:S(2)}, u32[]{:S(2)}) collective-permute-start(bf16[192,256]{1,0:T(8,128)(2,1)S(1)} %get-tuple-element.72), channel_id=1, source_target_pairs={{0,1},{1,2},{2,3},{3,0},{4,5},{5,6},{6,7},{7,4},{8,9},{9,10},{10,1... | collective-permute-start | bytes 294920 | tf_op jit(solution)/shard_map/ppermute | solution.py:26
  237.9 8.7 %collective-permute-start.6 = (bf16[192,256]{1,0:T(8,128)(2,1)S(1)}, bf16[192,256]{1,0:T(8,128)(2,1)S(1)}, u32[]{:S(2)}, u32[]{:S(2)}) collective-permute-start(bf16[192,256]{1,0:T(8,128)(2,1)S(1)} %get-tuple-element.68), channel_id=1, source_target_pairs={{0,1},{1,2},{2,3},{3,0},{4,5},{5,6},{6,7},{7,4},{8,9},{9,10},{10,1... | collective-permute-start | bytes 294920 | tf_op jit(solution)/shard_map/ppermute | solution.py:26
  240.5 8.6 %collective-permute-start.7 = (bf16[192,256]{1,0:T(8,128)(2,1)S(1)}, bf16[192,256]{1,0:T(8,128)(2,1)S(1)}, u32[]{:S(2)}, u32[]{:S(2)}) collective-permute-start(bf16[192,256]{1,0:T(8,128)(2,1)S(1)} %get-tuple-element.68), channel_id=1, source_target_pairs={{0,2},{1,3},{2,0},{3,1},{4,6},{5,7},{6,4},{7,5},{8,10},{9,11},{10,... | collective-permute-start | bytes 294920 | tf_op jit(solution)/shard_map/ppermute | solution.py:26
  243.0 11.1 %collective-permute-start.8 = (bf16[192,256]{1,0:T(8,128)(2,1)S(1)}, bf16[192,256]{1,0:T(8,128)(2,1)S(1)}, u32[]{:S(2)}, u32[]{:S(2)}) collective-permute-start(bf16[192,256]{1,0:T(8,128)(2,1)S(1)} %get-tuple-element.68), channel_id=1, source_target_pairs={{0,3},{1,0},{2,1},{3,2},{4,7},{5,4},{6,5},{7,6},{8,11},{9,8},{10,9... | collective-permute-start | bytes 294920 | tf_op jit(solution)/shard_map/ppermute | solution.py:26
Sparse Core Ops, SparseCore 0:
  9.9 116.7 all-gather.1

commit v2 on v0

v2 whole, which is shorter than its diff:
```python
import jax
import jax.numpy as jnp
from jax import lax
from jax.experimental import pallas as pl
from jax.experimental.pallas import tpu as pltpu
from jax.sharding import PartitionSpec as P

E = 128
K1 = 8
K2 = 4
HB = 32
NT = 64
N_REP = 4
BF = jnp.bfloat16
F32 = jnp.float32


def silu_slope(value):
    squash = jax.nn.sigmoid(value)
    return squash * (1.0 + value * (1.0 - squash))


def exchange(parts):
    return lax.all_to_all(parts, "table", split_axis=0, concat_axis=0, tiled=True)


def from_sibling(value):
    return lax.ppermute(value, "table", [(i, i ^ 1) for i in range(NT)])


def one_hot_rows(shape, source):
    row = lax.broadcasted_iota(jnp.int32, shape, 0)
    col = lax.broadcasted_iota(jnp.int32, shape, 1)
    return (source(row) == col).astype(F32).astype(BF)


def move_rows(order, rows):
    return jnp.dot(order, rows, preferred_element_type=F32).astype(BF)


def to_pieces(row):
    return ((row >> 1) & 3) * E + (row >> 3) * 2 + (row & 1)


def to_blocks(row):
    return ((row & 127) >> 1) * 8 + (row >> 7) * 2 + (row & 1)


def lift_kernel(got_ref, pooled_ref, u_ref, bias_ref, lifted_ref, factor_ref, terms_ref, weight_ref):
    weight = move_rows(one_hot_rows((512, 512), to_blocks), got_ref[:, 256:384])
    weight_ref[...] = weight
    factor = jnp.dot(got_ref[:, :256], u_ref[...], preferred_element_type=F32) + bias_ref[...] + 1.0
    factor_ref[...] = factor
    lifted = (pooled_ref[...].astype(F32) * factor).astype(BF)
    lifted_ref[...] = lifted
    for q in range(4):
        cols = slice(q * E, (q + 1) * E)
        terms_ref[:, cols] = jnp.dot(
            lifted[:, cols], weight[cols], preferred_element_type=F32
        ).astype(BF)


def whole(shape):
    return pl.BlockSpec(shape, lambda i: (0,) * len(shape))


def call(kernel, shapes, *values):
    return pl.pallas_call(
        kernel,
        grid=(1,),
        out_shape=shapes,
        in_specs=[whole(value.shape) for value in values],
        out_specs=[whole(shape.shape) for shape in shapes],
        compiler_params=pltpu.CompilerParams(vmem_limit_bytes=48 * 1024 * 1024),
    )(*values)


def lift(got, pooled, cross_u, bias):
    shapes = [((512, 512), BF), ((512, 512), F32), ((512, 512), BF), ((512, E), BF)]
    return call(
        lift_kernel,
        [jax.ShapeDtypeStruct(*shape) for shape in shapes],
        got,
        pooled,
        cross_u,
        bias,
    )


def first_kernel(got_ref, adds_ref, bias_ref, preact_ref, hidden_ref):
    total = jnp.broadcast_to(bias_ref[...][:, None, :], (HB, 8, E)).reshape(HB * 8, E)
    for q in range(4):
        total = total + jnp.dot(
            adds_ref[q], got_ref[:, q * E : (q + 1) * E], preferred_element_type=F32
        )
    preact_ref[...] = total
    hidden_ref[...] = (total * jax.nn.sigmoid(total)).astype(BF)


def hidden_first(got, adds, bias):
    return call(
        first_kernel,
        [jax.ShapeDtypeStruct((HB * 8, E), F32), jax.ShapeDtypeStruct((HB * 8, E), BF)],
        got,
        adds,
        bias,
    )


def start_kernel(pooled_ref, v_ref, weight_ref, pair_ref, out_ref):
    out_ref[:, :256] = jnp.dot(
        pooled_ref[...], v_ref[...], preferred_element_type=F32
    ).astype(BF)
    out_ref[:, 256:384] = move_rows(one_hot_rows((512, 512), to_pieces), weight_ref[...])
    pair = pair_ref[...]
    for i in range(32):
        out_ref[16 * i : 16 * i + 16, 384:] = pair


def regroup_kernel(got_ref, index_ref, extra_ref, out_ref):
    own = jnp.sum(got_ref[:, :256].astype(F32).reshape(NT, 8, 256), axis=0)
    own = jnp.concatenate([own, extra_ref[...]], axis=1) if extra_ref is not None else own
    width = own.shape[1]
    out_ref[:, :width] = (
        jnp.broadcast_to(own[None], (NT, 8, width)).reshape(512, width).astype(BF)
    )
    row = lax.broadcasted_iota(jnp.int32, (512, 512), 0)
    col = lax.broadcasted_iota(jnp.int32, (512, 512), 1)
    order = (index_ref[...] == (col >> 1)) & ((row & 1) == (col & 1))
    out_ref[:, width:] = move_rows(order.astype(F32).astype(BF), got_ref[:, 256:384])


def regroup(got, index, extra=None):
    kernel = regroup_kernel if extra is not None else (
        lambda got_ref, index_ref, out_ref: regroup_kernel(got_ref, index_ref, None, out_ref)
    )
    values = (got, index) if extra is None else (got, index, extra)
    width = 384 if extra is None else 512
    return pl.pallas_call(
        kernel,
        grid=(1,),
        out_shape=jax.ShapeDtypeStruct((512, width), BF),
        in_specs=[pl.BlockSpec((512, 384), lambda i: (0, 0))]
        + [pl.BlockSpec(value.shape, lambda i: (0, 0)) for value in values[1:]],
        out_specs=pl.BlockSpec((512, width), lambda i: (0, 0)),
        compiler_params=pltpu.CompilerParams(vmem_limit_bytes=48 * 1024 * 1024),
    )(*values)


def contract(left, right, at):
    return lax.dot_general(left, right, (((at,), (at,)), ((), ())), preferred_element_type=F32)


def owner_kernel(
    got_ref,
    weight_ref,
    lifted_ref,
    pooled_ref,
    factor_ref,
    crossed_ref,
    u_ref,
    sent_ref,
    direct_ref,
    up_ref,
    two_ref,
    vector_ref,
    bias_ref,
):
    crossed = crossed_ref[:, :256]
    back = jnp.zeros((512, 256), F32)
    blocks = []
    bias_ref[...] = jnp.zeros_like(bias_ref)
    for q in range(4):
        cols = slice(q * E, (q + 1) * E)
        rows = got_ref[:, cols]
        lifted_grad = contract(rows, weight_ref[cols, :], 1).astype(BF).astype(F32)
        cross_grad = lifted_grad * pooled_ref[:, cols].astype(F32)
        cross_half = cross_grad.astype(BF)
        direct_ref[:, cols] = lifted_grad * factor_ref[:, cols]
        back = back + contract(cross_half, u_ref[:, cols], 1)
        blocks.append(contract(lifted_ref[:, cols], rows, 0).astype(BF))
        up_ref[:, cols] = contract(crossed, cross_half, 0).astype(BF)
        bias_ref[q : q + 1, :] = jnp.sum(cross_grad, axis=0, keepdims=True)
    sent_ref[:, :256] = back.astype(BF)
    sent_ref[:, 256:] = move_rows(
        one_hot_rows((512, 512), to_pieces), jnp.concatenate(blocks, axis=0)
    )
    two_rows = got_ref[:, 6 * E : 7 * E]
    two_ref[...] = contract(got_ref[:, 4 * E : 6 * E], two_rows, 0).astype(BF)
    vector_ref[...] = jnp.concatenate(
        [
            jnp.sum(two_rows.astype(F32), axis=0, keepdims=True),
            jnp.sum(got_ref[:, 7 * E :].astype(F32), axis=0, keepdims=True),
            jnp.zeros((6, E), F32),
        ],
        axis=0,
    )


QUARTER = 368


def late_kernel(got_ref, pooled_ref, up_ref, two_ref, bias_ref, late_ref):
    local_v = contract(pooled_ref[...], got_ref[:, :256], 0).astype(BF)
    blocks = move_rows(one_hot_rows((512, 512), to_blocks), got_ref[:, 384:])

    def vector_source(row):
        place = (row >> 5) * 24 + (row & 31)
        which = place >> 5
        hidden = place & 31
        return 16 * hidden + jnp.where(which == 2, 8, 0) + jnp.where(which == 1, 0, 1)

    order = one_hot_rows((E, 512), vector_source)
    vectors = jnp.dot(order, got_ref[:, 256:384], preferred_element_type=F32)
    in_quarter = lax.broadcasted_iota(jnp.int32, (32, E), 0)
    for k in range(4):
        base = QUARTER * k
        late_ref[base : base + 128, :] = local_v[128 * k : 128 * k + 128]
        small = vectors[32 * k : 32 * k + 32]
        small = jnp.where(in_quarter == 24, bias_ref[k : k + 1, :], small).astype(BF)
        for side in range(2):
            cols = slice(side * E, (side + 1) * E)
            at = 128 * k + 64 * side
            late_ref[base + 128 : base + 192, cols] = blocks[at : at + 64]
            late_ref[base + 192 : base + 208, cols] = small[16 * side : 16 * side + 16]
            at = base + 208 + 64 * side
            late_ref[at : at + 64, :] = up_ref[64 * k : 64 * k + 64, 256 * side : 256 * side + 256]
            at = 64 * k + 32 * side
            late_ref[base + 336 : base + 368, cols] = two_ref[at : at + 32, :]


def add_kernel(got_ref, out_ref):
    total = got_ref[:QUARTER, :].astype(F32)
    for k in range(1, 4):
        total = total + got_ref[QUARTER * k : QUARTER * (k + 1), :].astype(F32)
    for k in range(4):
        out_ref[QUARTER * k : QUARTER * (k + 1), :] = total.astype(BF)


def last_kernel(got_ref, v_ref, one_ref, small_ref, up_ref, two_ref):
    for k in range(4):
        base = QUARTER * k
        v_ref[128 * k : 128 * k + 128, :] = got_ref[base : base + 128, :].astype(F32)
        for side in range(2):
            cols = slice(side * E, (side + 1) * E)
            at = 128 * k + 64 * side
            one_ref[at : at + 64, :] = got_ref[base + 128 : base + 192, cols].astype(F32)
            at = 32 * k + 16 * side
            small_ref[at : at + 16, :] = got_ref[base + 192 : base + 208, cols].astype(F32)
            at = base + 208 + 64 * side
            up_ref[64 * k : 64 * k + 64, 256 * side : 256 * side + 256] = got_ref[
                at : at + 64, :
            ].astype(F32)
            at = 64 * k + 32 * side
            two_ref[at : at + 32, :] = got_ref[base + 336 : base + 368, cols].astype(F32)


def body(
    pooled,
    table_slot,
    cross_v,
    cross_u,
    cross_bias,
    block_index1,
    weight1,
    block_index2,
    weight2,
    top_vectors,
    labels,
    importance,
):
    tables = table_slot.shape[0]
    contract_last = (((1,), (1,)), ((), ()))
    core = lax.axis_index("table") % 2
    half_index = lax.dynamic_index_in_dim(block_index2.reshape(HB, 2, 2), core, 2, keepdims=False)
    half_index = half_index.reshape(-1)

    reads = block_index1[:, None] == table_slot[None, :]
    numbers = jnp.arange(tables, dtype=jnp.int32)
    block_of_slot = jnp.sum(jnp.where(reads, numbers[:, None], 0), axis=0)
    slot_of_block = jnp.sum(jnp.where(reads, numbers[None, :], 0), axis=1)
    block_of_slot = jnp.repeat(block_of_slot, 2)[:, None]
    slot_of_block = jnp.repeat(slot_of_block, 2)[:, None]
    hidden_of_slot = jnp.sum(
        jnp.where(reads, jnp.arange(tables, dtype=jnp.int32)[:, None] // K1, 0), axis=0
    )
    out_row = lax.broadcasted_iota(jnp.int32, (4, HB * 8, NT * 8), 1)
    in_row = lax.broadcasted_iota(jnp.int32, (4, HB * 8, NT * 8), 2)
    wanted = jnp.repeat(hidden_of_slot.reshape(NT, 4).T, 8, axis=1)[:, None, :]
    adds = ((wanted == out_row // 8) & (out_row % 8 == in_row % 8)).astype(BF)

    pair_two = weight2.reshape(2, 16, 8, E).transpose(0, 2, 1, 3).reshape(16, 16 * E)
    (sent,) = call(
        start_kernel,
        [jax.ShapeDtypeStruct((512, 2432), BF)],
        pooled,
        cross_v,
        weight1.reshape(512, E),
        pair_two,
    )
    got = exchange(sent.reshape(NT, 8, 2432))
    half_two = got[:, :, 384:].reshape(NT, 8, 16, E).transpose(0, 2, 1, 3).reshape(NT, E, E)
    sent = regroup(got.reshape(512, 2432), block_of_slot)
    arrived = exchange(sent.reshape(NT, 8, 384)).reshape(512, 384)
    lifted, factor, terms, weight_slot = lift(
        arrived, pooled, cross_u, cross_bias.reshape(1, 512)
    )
    got = exchange(terms.reshape(NT, 8, 512))
    preact_one, hidden_one = hidden_first(
        got.reshape(512, 512), adds, top_vectors[0].reshape(HB, E)
    )
    preact_one = preact_one.reshape(HB, 8, E).transpose(1, 0, 2)
    hidden_one = hidden_one.reshape(HB, 8, E).transpose(1, 0, 2)
    hidden_both = jnp.concatenate([hidden_one, from_sibling(hidden_one)], axis=0)
    picked_both = hidden_both[:, half_index]
    terms_two = jnp.einsum("bnc,ncd->bnd", picked_both, half_two, preferred_element_type=F32)
    half_sum = terms_two.reshape(16, HB, 2, E).sum(axis=2)
    preact_two = half_sum[:8] + from_sibling(half_sum[8:]) + top_vectors[1].reshape(-1, E)
    hidden_two = jax.nn.silu(preact_two).astype(BF)
    last_weight = top_vectors[2].reshape(-1, E)
    logit = jnp.sum(hidden_two.astype(F32) * last_weight, axis=(1, 2))
    sample_weight = importance.reshape(-1).astype(F32) / 8.0
    targets = labels.reshape(-1).astype(F32)
    grad_logit = sample_weight * (jax.nn.sigmoid(logit) - targets)
    grad_two = (grad_logit[:, None, None] * last_weight * silu_slope(preact_two)).astype(BF)
    last_terms = (hidden_two.astype(F32) * grad_logit[:, None, None]).astype(BF)
    grad_both = jnp.concatenate([grad_two, from_sibling(grad_two)], axis=0)
    spread_two = jnp.repeat(grad_both, 2, axis=1)
    back_two = jnp.einsum("bnd,ncd->bnc", spread_two, half_two, preferred_element_type=F32)
    onehot_two = (half_index[:, None] == jnp.arange(HB, dtype=jnp.int32)[None, :]).astype(F32)
    half_into = jnp.einsum("bnc,nj->bjc", back_two, onehot_two, precision=lax.Precision.HIGHEST)
    into_one = half_into[:8] + from_sibling(half_into[8:])
    grad_one = (into_one * silu_slope(preact_one)).astype(BF)

    spread_one = grad_one[:, hidden_of_slot].reshape(8, NT, 4 * E)
    picked_pair = hidden_one[:, block_index2].reshape(8, NT, 2 * E)
    both = jnp.repeat(grad_two, 2, axis=1)
    third = jnp.stack([grad_one, last_terms], axis=2).reshape(8, NT, E)
    sent = jnp.concatenate([spread_one, picked_pair, both, third], axis=2).transpose(1, 0, 2)
    got = exchange(sent).reshape(512, 8 * E)
    sent, direct, local_u, local_two, vector_rows, local_bias = call(
        owner_kernel,
        [
            jax.ShapeDtypeStruct((512, 384), BF),
            jax.ShapeDtypeStruct((512, 512), F32),
            jax.ShapeDtypeStruct((256, 512), BF),
            jax.ShapeDtypeStruct((256, E), BF),
            jax.ShapeDtypeStruct((8, E), F32),
            jax.ShapeDtypeStruct((8, E), F32),
        ],
        got,
        weight_slot,
        lifted,
        pooled,
        factor,
        arrived,
        cross_u,
    )
    got = exchange(sent.reshape(NT, 8, 384))
    sent = regroup(got.reshape(512, 384), slot_of_block, vector_rows)
    got = exchange(sent.reshape(NT, 8, 512)).reshape(512, 512)
    grad_crossed = got[:, :256]
    parts = [jax.ShapeDtypeStruct((4 * QUARTER, 256), BF)]
    (late,) = call(late_kernel, parts, got, pooled, local_u, local_two, local_bias)
    late = lax.all_to_all(late, "rep", split_axis=0, concat_axis=0, tiled=True)
    (late,) = call(add_kernel, parts, late)
    late = lax.all_to_all(late, "rep", split_axis=0, concat_axis=0, tiled=True)
    shapes = [(512, 256), (512, E), (E, E), (256, 512), (256, E)]
    grad_v, grad_w1, small, grad_u, grad_w2 = call(
        last_kernel, [jax.ShapeDtypeStruct(shape, F32) for shape in shapes], late
    )
    d_pooled = (
        direct + lax.dot_general(grad_crossed, cross_v, contract_last, preferred_element_type=F32)
    ).astype(BF)

    grad_w1 = grad_w1.reshape(4, E, E)
    grad_w2 = grad_w2.reshape(2, E, E)
    small = small.reshape(4, 32, E)
    grad_bias = small[:, 24].reshape(512)
    grad_vectors = small[:, :24].reshape(3, HB * E)
    return (d_pooled, grad_v, grad_u, grad_bias, grad_w1, grad_w2, grad_vectors)


def solution(mesh):
    placed = (
        P("rep", "table"),
        P(),
        P("table", None),
        P(None, "table"),
        P("table"),
        P(),
        P("table", None, None),
        P(),
        P("table", None, None),
        P(),
        P("rep", "table"),
        P("rep", "table"),
    )
    return jax.shard_map(
        body,
        mesh=mesh,
        in_specs=placed,
        out_specs=(
            P("rep", "table"),
            P("table", None),
            P(None, "table"),
            P("table"),
            P("table", None, None),
            P("table", None, None),
            P(),
        ),
        check_vma=False,
    )
```

time: 1050 us -> 227 us (0.22)
  blocking collectives: 662 us -> 67.5 us
  waiting for transfers between devices: 300 us -> 78.7 us
  matrix products: 39.9 us -> 5.64 us
  starting transfers between devices: 16 us -> 32.3 us
  local copies, waits for them, and re-layouts: 8.56 us -> 24 us
  between operations: 14 us -> 1.18 us
    psum x4 -> x0, blocking collectives: 642 us -> none  [the longest x1 273 us: body(): crossed = lax.psum(partial_sum, 'table').astype(jnp.bfloat16)]
    reduce_scatter x2 -> x0, waiting for transfers between devices: 293 us -> none  [the longest x1 293 us: body(): lax.psum_scatter(local_one, 'table', scatter_dimension=0, tiled=True)]
    all_to_all x1 -> x5, waiting for transfers between devices: 5.35 us -> 76.8 us  [the longest x4 59.4 us: exchange(): lax.all_to_all(parts, 'table', split_axis=0, concat_axis=0, tiled=True)]
    all_to_all x1 -> x3, blocking collectives: 19.3 us -> 67.5 us  [the longest x2 39.3 us: exchange(): lax.all_to_all(parts, 'table', split_axis=0, concat_axis=0, tiled=True)]
    dot_general x12 -> x2, matrix products: 37.5 us -> 2.81 us  [the longest x1 1.62 us: body(): jnp.einsum('bnc,ncd->bnd', picked_both, half_two, preferred_element_type=...]
    all_to_all x1 -> x5, starting transfers between devices: 15.7 us -> 31.5 us  [the longest x4 28 us: exchange(): lax.all_to_all(parts, 'table', split_axis=0, concat_axis=0, tiled=True)]
    unnamed x11 -> x71, local copies, waits for them, and re-layouts: 1.91 us -> 14 us
  transfers between devices with their start and end apart: 6 -> 9, of which waited for: 2 -> 7; matrix products, arithmetic and copies ran while one was open for 4% -> 5% of each run, Pallas kernels for 0% -> 0%
where the time goes in v2:
time: 227 us; the launch traced here: 226 us
  waiting for transfers between devices  78.7 us (35%)
  blocking collectives  67.5 us (30%)
  starting transfers between devices  32.3 us (14%)
  local copies, waits for them, and re-layouts  24 us (11%)
  other arithmetic  8.67 us (4%)
  Pallas kernels  8.12 us (4%)
  matrix products  5.64 us (2%)
    all_to_all x4, waiting for transfers between devices, exchange(): lax.all_to_all(parts, 'table', split_axis=0, concat_axis=0, tiled=True)  59.4 us
    all_to_all x2, blocking collectives, exchange(): lax.all_to_all(parts, 'table', split_axis=0, concat_axis=0, tiled=True)  39.3 us
    all_to_all x1, blocking collectives, body(): late = lax.all_to_all(late, 'rep', split_axis=0, concat_axis=0, tiled=True)  28.2 us
    all_to_all x4, starting transfers between devices, exchange(): lax.all_to_all(parts, 'table', split_axis=0, concat_axis=0, tiled=True)  28 us
    all_to_all x1, waiting for transfers between devices, body(): late = lax.all_to_all(late, 'rep', split_axis=0, concat_axis=0, tiled=True)  17.4 us
    unnamed x71, local copies, waits for them, and re-layouts  14 us
    pallas_call x7, Pallas kernels, call(): pl.pallas_call(kernel, grid=(1,), out_shape=shapes, in_specs=[whole(value...  7.33 us
  transfers between devices with their start and end apart: 9, of which 7 were waited for; matrix products, arithmetic and copies ran while one was open for 5% of the time, Pallas kernels for 0%

profile of v2, /device:TPU:2, one launch (start us, length us, event | category | flops | bytes accessed | tf_op | source)
XLA Modules:
  0.0 226.1 jit_solution(14478803695006486674)
XLA Ops:
  0.6 1.0 copy-done.1
  1.7 0.9 copy-done.9
  2.6 0.9 copy-done.19
  3.5 0.8 copy-done.20
  4.4 0.5 shard_map.171
  4.9 1.4 copy-done
  6.4 9.5 %all-to-all-start = ((bf16[64,8,2432]{2,1,0:T(8,128)(2,1)}), bf16[64,8,2432]{2,1,0:T(8,128)(2,1)S(1)}, u32[]{:S(2)}, u32[]{:S(2)}) async-start(bf16[64,8,2432]{2,1,0:T(8,128)(2,1)} %bitcast.104), calls=%async_computation | async-start | bytes 4980736 | tf_op jit(solution)/shard_map/all_to_all | solution.py:24
  15.9 0.8 fusion.9
  16.8 0.8 broadcast_in_dim_reshape.10.index_ref
  18.2 0.7 dynamic-slice_reduce_fusion
  19.0 29.4 %all-to-all-done = bf16[64,8,2432]{2,1,0:T(8,128)(2,1)S(1)} async-done(((bf16[64,8,2432]{2,1,0:T(8,128)(2,1)}), bf16[64,8,2432]{2,1,0:T(8,128)(2,1)S(1)}, u32[]{:S(2)}, u32[]{:S(2)}) %all-to-all-start) | async-done | bytes 2490400 | tf_op jit(solution)/shard_map/all_to_all | solution.py:24
  48.4 0.9 copy-done.5
  49.3 0.4 shard_map.172
  49.7 0.7 copy-done.4
  50.5 6.4 %all-to-all-start.1 = ((bf16[64,8,384]{2,1,0:T(8,128)(2,1)}), bf16[64,8,384]{2,1,0:T(8,128)(2,1)S(1)}, u32[]{:S(2)}, u32[]{:S(2)}) async-start(bf16[64,8,384]{2,1,0:T(8,128)(2,1)} %bitcast.117), calls=%async_computation.1 | async-start | bytes 786432 | tf_op jit(solution)/shard_map/all_to_all | solution.py:24
  57.0 1.3 fusion.1.adds_ref
  58.3 9.0 %all-to-all-done.1 = bf16[64,8,384]{2,1,0:T(8,128)(2,1)S(1)} async-done(((bf16[64,8,384]{2,1,0:T(8,128)(2,1)}), bf16[64,8,384]{2,1,0:T(8,128)(2,1)S(1)}, u32[]{:S(2)}, u32[]{:S(2)}) %all-to-all-start.1) | async-done | bytes 393248 | tf_op jit(solution)/shard_map/all_to_all | solution.py:24
  67.3 0.9 copy-done.11
  68.2 0.6 shard_map.173
  68.9 1.0 copy-done.7
  69.8 0.8 copy-done.13
  70.6 0.8 copy-done.15
  71.4 0.7 copy-done.16
  72.1 6.4 %all-to-all-start.2 = ((bf16[64,8,512]{2,1,0:T(8,128)(2,1)}), bf16[64,8,512]{2,1,0:T(8,128)(2,1)}, u32[]{:S(2)}, u32[]{:S(2)}) async-start(bf16[64,8,512]{2,1,0:T(8,128)(2,1)} %bitcast.119), calls=%async_computation.2 | async-start | bytes 1048576 | tf_op jit(solution)/shard_map/all_to_all | solution.py:24
  78.5 1.0 fusion.39
  79.5 10.7 %all-to-all-done.2 = bf16[64,8,512]{2,1,0:T(8,128)(2,1)} async-done(((bf16[64,8,512]{2,1,0:T(8,128)(2,1)}), bf16[64,8,512]{2,1,0:T(8,128)(2,1)}, u32[]{:S(2)}, u32[]{:S(2)}) %all-to-all-start.2) | async-done | bytes 524320 | tf_op jit(solution)/shard_map/all_to_all | solution.py:24
  90.2 1.2 copy-done.3
  91.4 1.5 shard_map.174
  92.9 0.6 copy-done.18
  93.6 1.2 collective-permute-done
  94.8 0.7 pad_maximum_fusion
  95.5 2.3 gather_fusion
  97.8 1.6 bitcast_reduce_fusion
  99.5 0.2 collective-permute-start.1
  99.7 0.6 compare_select_fusion.3
  100.3 0.6 collective-permute-done.1
  100.9 0.2 fusion.14
  101.1 1.5 multiply_convert_fusion
  102.7 0.6 compare_select_fusion.4
  103.3 0.6 eq.46
  103.9 0.9 pad_maximum_fusion.1
  104.9 1.2 fusion.5
  106.1 0.5 convolution_bitcast_fusion
  106.6 0.4 collective-permute-start.3
  107.1 1.4 gather_fusion.2
  108.5 1.0 fusion.17
  109.6 0.8 gather_fusion.1
  110.5 1.2 maximum_bitcast_fusion
  111.8 22.4 %all_to_all.52 = bf16[64,8,1024]{2,1,0:T(8,128)(2,1)S(1)} all-to-all(bf16[64,8,1024]{2,1,0:T(8,128)(2,1)S(1)} %maximum_bitcast_fusion), channel_id=1, replica_groups=mesh['table'=64,'rep'=4] {'table'}, dimensions={0} | all-to-all | bytes 2097152 | tf_op jit(solution)/shard_map/all_to_all | solution.py:24
  134.2 2.2 shard_map.175
  136.4 1.0 copy-done.6
  137.4 5.7 %all-to-all-start.4 = ((bf16[64,8,384]{2,1,0:T(8,128)(2,1)}), bf16[64,8,384]{2,1,0:T(8,128)(2,1)S(1)}, u32[]{:S(2)}, u32[]{:S(2)}) async-start(bf16[64,8,384]{2,1,0:T(8,128)(2,1)} %bitcast.47), calls=%async_computation.4 | async-start | bytes 786432 | tf_op jit(solution)/shard_map/all_to_all | solution.py:24
  143.3 10.2 %all-to-all-done.4 = bf16[64,8,384]{2,1,0:T(8,128)(2,1)S(1)} async-done(((bf16[64,8,384]{2,1,0:T(8,128)(2,1)}), bf16[64,8,384]{2,1,0:T(8,128)(2,1)S(1)}, u32[]{:S(2)}, u32[]{:S(2)}) %all-to-all-start.4) | async-done | bytes 393248 | tf_op jit(solution)/shard_map/all_to_all | solution.py:24
  153.5 0.4 shard_map.176
  153.9 16.9 %all_to_all.53 = bf16[64,8,512]{2,1,0:T(8,128)(2,1)S(1)} all-to-all(bf16[64,8,512]{2,1,0:T(8,128)(2,1)S(1)} %bitcast.113), channel_id=1, replica_groups=mesh['table'=64,'rep'=4] {'table'}, dimensions={0} | all-to-all | bytes 1048576 | tf_op jit(solution)/shard_map/all_to_all | solution.py:24
  170.8 0.5 shard_map.177
  171.3 28.2 %all_to_all.54 = bf16[4,368,256]{2,1,0:T(8,128)(2,1)S(1)} all-to-all(bf16[4,368,256]{2,1,0:T(8,128)(2,1)S(1)} %bitcast.111), channel_id=1, replica_groups=mesh['table'=64,'rep'=4] {'rep'}, dimensions={0} | all-to-all | bytes 1507328 | tf_op jit(solution)/shard_map/all_to_all | solution.py:365
  199.5 1.0 shard_map.178
  200.5 3.5 %all-to-all-start.7 = ((bf16[4,368,256]{2,1,0:T(8,128)(2,1)}), bf16[4,368,256]{2,1,0:T(8,128)(2,1)S(1)}, u32[]{:S(2)}, u32[]{:S(2)}) async-start(bf16[4,368,256]{2,1,0:T(8,128)(2,1)} %bitcast.53), calls=%async_computation.7 | async-start | bytes 1507328 | tf_op jit(solution)/shard_map/all_to_all | solution.py:367
  204.0 2.4 %fusion.4 = bf16[512,512]{1,0:T(8,128)(2,1)} fusion(f32[512,512]{1,0:T(8,128)} %copy-done.6, bf16[512,256]{1,0:T(8,128)(2,1)S(1)} %copy-done.10, bf16[512,512]{1,0:T(8,128)(2,1)S(1)} %bitcast.109), kind=kOutput, calls=%fused_computation.11 | convolution fusion | flops 134742016 | bytes 2097152 | tf_op jit(solution)/shard_map/dot_general | solution.py:373
  206.3 17.4 %all-to-all-done.7 = bf16[4,368,256]{2,1,0:T(8,128)(2,1)S(1)} async-done(((bf16[4,368,256]{2,1,0:T(8,128)(2,1)}), bf16[4,368,256]{2,1,0:T(8,128)(2,1)S(1)}, u32[]{:S(2)}, u32[]{:S(2)}) %all-to-all-start.7) | async-done | bytes 753696 | tf_op jit(solution)/shard_map/all_to_all | solution.py:367
  223.7 1.1 shard_map.179
  224.8 0.6 slice.56
  225.4 0.7 reshape.256
  (90 shorter events, 1.6 us)
Async XLA Ops:
  0.6 1.0 copy-start.1
  1.7 0.9 copy-start.9
  2.6 0.9 copy-start.19
  3.5 0.8 copy-start.20
  4.9 1.4 copy-start
  6.4 9.6 %copy-start.28 = (s32[256]{0:T(256)S(1)}, s32[256]{0:T(256)}, u32[]{:S(2)}) copy-start(s32[256]{0:T(256)} %param.13) | copy-start | bytes 3076
  6.4 9.6 %copy-start.29 = (s32[256]{0:T(256)S(1)}, s32[256]{0:T(256)}, u32[]{:S(2)}) copy-start(s32[256]{0:T(256)} %param.17) | copy-start | bytes 3076
  6.4 11.7 %copy-start.30 = (s32[128]{0:T(128)S(1)}, s32[128]{0:T(128)}, u32[]{:S(2)}) copy-start(s32[128]{0:T(128)} %param.19) | copy-start | bytes 1540
  6.4 42.0 %all-to-all-start = ((bf16[64,8,2432]{2,1,0:T(8,128)(2,1)}), bf16[64,8,2432]{2,1,0:T(8,128)(2,1)S(1)}, u32[]{:S(2)}, u32[]{:S(2)}) async-start(bf16[64,8,2432]{2,1,0:T(8,128)(2,1)} %bitcast.104), calls=%async_computation | async-start | bytes 4980736 | tf_op jit(solution)/shard_map/all_to_all | solution.py:24
  48.4 1.0 copy-start.5
  49.3 18.0 %copy-start.2 = (bf16[512,512]{1,0:T(8,128)(2,1)S(1)}, bf16[512,512]{1,0:T(8,128)(2,1)}, u32[]{:S(2)}) copy-start(bf16[512,512]{1,0:T(8,128)(2,1)} %pooled_ref.7) | copy-start | bytes 1572868
  49.3 18.0 %copy-start.21 = (f32[512]{0:T(512)S(1)}, f32[512]{0:T(512)}, u32[]{:S(2)}) copy-start(f32[512]{0:T(512)} %param.16) | copy-start | bytes 6148
  49.7 0.7 copy-start.4
  50.5 16.8 %all-to-all-start.1 = ((bf16[64,8,384]{2,1,0:T(8,128)(2,1)}), bf16[64,8,384]{2,1,0:T(8,128)(2,1)S(1)}, u32[]{:S(2)}, u32[]{:S(2)}) async-start(bf16[64,8,384]{2,1,0:T(8,128)(2,1)} %bitcast.117), calls=%async_computation.1 | async-start | bytes 786432 | tf_op jit(solution)/shard_map/all_to_all | solution.py:24
  67.3 1.0 copy-start.11
  68.9 1.0 copy-start.7
  69.8 0.8 copy-start.13
  70.6 0.8 copy-start.15
  71.4 0.7 copy-start.16
  72.1 18.1 %all-to-all-start.2 = ((bf16[64,8,512]{2,1,0:T(8,128)(2,1)}), bf16[64,8,512]{2,1,0:T(8,128)(2,1)}, u32[]{:S(2)}, u32[]{:S(2)}) async-start(bf16[64,8,512]{2,1,0:T(8,128)(2,1)} %bitcast.119), calls=%async_computation.2 | async-start | bytes 1048576 | tf_op jit(solution)/shard_map/all_to_all | solution.py:24
  79.5 21.4 %copy-start.23 = (f32[1,4096]{1,0:T(1,128)}, f32[1,4096]{1,0:T(1,128)S(1)}, u32[]{:S(2)}) copy-start(f32[1,4096]{1,0:T(1,128)S(1)} %get-tuple-element.49) | copy-start | bytes 49156
  79.5 21.4 %copy-start.24 = (f32[1,4096]{1,0:T(1,128)}, f32[1,4096]{1,0:T(1,128)S(1)}, u32[]{:S(2)}) copy-start(f32[1,4096]{1,0:T(1,128)S(1)} %get-tuple-element.50) | copy-start | bytes 49156
  90.2 1.2 copy-start.3
  92.9 0.7 copy-start.18
  93.6 1.3 collective-permute-start
  95.5 5.6 %copy-start.33 = (s32[1,8]{1,0:T(1,128)S(1)}, s32[1,8]{1,0:T(1,128)}, u32[]{:S(2)}) copy-start(s32[1,8]{1,0:T(1,128)} %param.22) | copy-start | bytes 100
  95.5 5.6 %copy-start.34 = (s32[1,8]{1,0:T(1,128)S(1)}, s32[1,8]{1,0:T(1,128)}, u32[]{:S(2)}) copy-start(s32[1,8]{1,0:T(1,128)} %param.23) | copy-start | bytes 100
  97.8 4.9 %copy-start.31 = (s32[128]{0:T(128)S(1)}, s32[128]{0:T(128)}, u32[]{:S(2)}) copy-start(s32[128]{0:T(128)} %param.19) | copy-start | bytes 1540
  99.5 1.4 collective-permute-start.1
  102.5 1.4 collective-permute-start.2
  103.9 2.2 copy-start.27
  104.9 2.2 copy-start.32
  104.9 2.2 copy-start.26
  106.1 3.4 %copy-start.22 = (bf16[8,32,1,128]{3,1,0,2:T(8,128)(2,1)S(1)}, bf16[8,32,1,128]{3,1,0,2:T(8,128)(2,1)}, u32[]{:S(2)}) copy-start(bf16[8,32,1,128]{3,1,0,2:T(8,128)(2,1)} %get-tuple-element.52) | copy-start | bytes 196612
  106.6 1.9 collective-permute-start.3
  110.5 23.7 %copy-start.8 = (f32[512,512]{1,0:T(8,128)S(1)}, f32[512,512]{1,0:T(8,128)}, u32[]{:S(2)}) copy-start(f32[512,512]{1,0:T(8,128)} %copy-done.7) | copy-start | bytes 3145732
  110.5 23.7 %copy-start.12 = (bf16[256,512]{1,0:T(8,128)(2,1)S(1)}, bf16[256,512]{1,0:T(8,128)(2,1)}, u32[]{:S(2)}) copy-start(bf16[256,512]{1,0:T(8,128)(2,1)} %u_ref.3) | copy-start | bytes 786436
  110.5 23.7 %copy-start.14 = (bf16[512,512]{1,0:T(8,128)(2,1)S(1)}, bf16[512,512]{1,0:T(8,128)(2,1)}, u32[]{:S(2)}) copy-start(bf16[512,512]{1,0:T(8,128)(2,1)} %copy-done.13) | copy-start | bytes 1572868
  110.5 23.7 %copy-start.17 = (bf16[512,128]{1,0:T(8,128)(2,1)S(1)}, bf16[512,128]{1,0:T(8,128)(2,1)}, u32[]{:S(2)}) copy-start(bf16[512,128]{1,0:T(8,128)(2,1)} %copy-done.16) | copy-start | bytes 393220
  134.2 8.8 %copy-start.25 = (s32[256]{0:T(256)S(1)}, s32[256]{0:T(256)}, u32[]{:S(2)}) copy-start(s32[256]{0:T(256)} %get-tuple-element.41) | copy-start | bytes 3076
  136.4 1.0 copy-start.6
  137.4 16.1 %all-to-all-start.4 = ((bf16[64,8,384]{2,1,0:T(8,128)(2,1)}), bf16[64,8,384]{2,1,0:T(8,128)(2,1)S(1)}, u32[]{:S(2)}, u32[]{:S(2)}) async-start(bf16[64,8,384]{2,1,0:T(8,128)(2,1)} %bitcast.47), calls=%async_computation.4 | async-start | bytes 786432 | tf_op jit(solution)/shard_map/all_to_all | solution.py:24
  171.3 32.7 %copy-start.10 = (bf16[512,256]{1,0:T(8,128)(2,1)S(1)}, bf16[512,256]{1,0:T(8,128)(2,1)}, u32[]{:S(2)}) copy-start(bf16[512,256]{1,0:T(8,128)(2,1)} %v_ref.1) | copy-start | bytes 786436
  200.5 23.3 %all-to-all-start.7 = ((bf16[4,368,256]{2,1,0:T(8,128)(2,1)}), bf16[4,368,256]{2,1,0:T(8,128)(2,1)S(1)}, u32[]{:S(2)}, u32[]{:S(2)}) async-start(bf16[4,368,256]{2,1,0:T(8,128)(2,1)} %bitcast.53), calls=%async_computation.7 | async-start | bytes 1507328 | tf_op jit(solution)/shard_map/all_to_all | solution.py:367

commit v3 on v2

--- a/solution.py
+++ b/solution.py
@@ -68,10 +68,10 @@
     return pl.pallas_call(
         kernel,
         grid=(1,),
-        out_shape=shapes,
+        out_shape=[pltpu.HBM(shape.shape, shape.dtype) for shape in shapes],
         in_specs=[whole(value.shape) for value in values],
         out_specs=[whole(shape.shape) for shape in shapes],
-        compiler_params=pltpu.CompilerParams(vmem_limit_bytes=48 * 1024 * 1024),
+        compiler_params=pltpu.CompilerParams(vmem_limit_bytes=24 * 1024 * 1024),
     )(*values)
 
 
@@ -139,11 +139,11 @@
     return pl.pallas_call(
         kernel,
         grid=(1,),
-        out_shape=jax.ShapeDtypeStruct((512, width), BF),
+        out_shape=pltpu.HBM((512, width), BF),
         in_specs=[pl.BlockSpec((512, 384), lambda i: (0, 0))]
         + [pl.BlockSpec(value.shape, lambda i: (0, 0)) for value in values[1:]],
         out_specs=pl.BlockSpec((512, width), lambda i: (0, 0)),
-        compiler_params=pltpu.CompilerParams(vmem_limit_bytes=48 * 1024 * 1024),
+        compiler_params=pltpu.CompilerParams(vmem_limit_bytes=24 * 1024 * 1024),
     )(*values)
 
 

time: 227 us -> 227 us (level)
  local copies, waits for them, and re-layouts: 24 us -> 16.5 us
  Pallas kernels: 8.12 us -> 14.3 us
    unnamed x71, local copies, waits for them, and re-layouts: 14 us -> 6.74 us
    pallas_call x9, Pallas kernels: 8.12 us -> 14.3 us  [the longest x7 12 us: call(): pl.pallas_call(kernel, grid=(1,), out_shape=[pltpu.HBM(shape.shape, shape...]
  transfers between devices with their start and end apart: 9 -> 9, of which waited for: 7 -> 7; matrix products, arithmetic and copies ran while one was open for 5% -> 4% of each run, Pallas kernels for 0% -> 0%
where the time goes in v3:
time: 227 us; the launch traced here: 226 us
  waiting for transfers between devices  80.6 us (36%)
  blocking collectives  68.3 us (30%)
  starting transfers between devices  32.6 us (14%)
  local copies, waits for them, and re-layouts  16.5 us (7%)
  Pallas kernels  14.3 us (6%)
  other arithmetic  7.8 us (3%)
  matrix products  4.45 us (2%)
    all_to_all x4, waiting for transfers between devices, exchange(): lax.all_to_all(parts, 'table', split_axis=0, concat_axis=0, tiled=True)  60.4 us
    all_to_all x2, blocking collectives, exchange(): lax.all_to_all(parts, 'table', split_axis=0, concat_axis=0, tiled=True)  39.9 us
    all_to_all x1, blocking collectives, body(): late = lax.all_to_all(late, 'rep', split_axis=0, concat_axis=0, tiled=True)  28.4 us
    all_to_all x4, starting transfers between devices, exchange(): lax.all_to_all(parts, 'table', split_axis=0, concat_axis=0, tiled=True)  28.2 us
    all_to_all x1, waiting for transfers between devices, body(): late = lax.all_to_all(late, 'rep', split_axis=0, concat_axis=0, tiled=True)  18.6 us
    pallas_call x7, Pallas kernels, call(): pl.pallas_call(kernel, grid=(1,), out_shape=[pltpu.HBM(shape.shape, shape...  12 us
    unnamed x71, local copies, waits for them, and re-layouts  6.74 us
  transfers between devices with their start and end apart: 9, of which 7 were waited for; matrix products, arithmetic and copies ran while one was open for 4% of the time, Pallas kernels for 0%

profile of v3, /device:TPU:2, one launch (start us, length us, event | category | flops | bytes accessed | tf_op | source)
XLA Modules:
  0.0 225.5 jit_solution(11798643955106327167)
XLA Ops:
  0.6 1.0 copy-done
  1.7 0.9 copy-done.4
  2.6 0.9 copy-done.11
  3.5 0.8 copy-done.12
  4.4 2.0 shard_map.171
  6.4 9.5 %all-to-all-start = ((bf16[64,8,2432]{2,1,0:T(8,128)(2,1)}), bf16[64,8,2432]{2,1,0:T(8,128)(2,1)S(1)}, u32[]{:S(2)}, u32[]{:S(2)}) async-start(bf16[64,8,2432]{2,1,0:T(8,128)(2,1)} %bitcast.116), calls=%async_computation | async-start | bytes 4980736 | tf_op jit(solution)/shard_map/all_to_all | solution.py:24
  15.9 0.8 fusion.9
  16.8 0.1 broadcast_in_dim_reshape.10.index_ref
  16.9 0.1 reshape.238
  17.1 0.1 broadcast_in_dim.60
  17.2 0.1 eq.53
  17.3 0.2 reshape.225
  17.5 0.7 dynamic-slice_reduce_fusion
  18.2 0.1 reshape.240
  18.3 30.1 %all-to-all-done = bf16[64,8,2432]{2,1,0:T(8,128)(2,1)S(1)} async-done(((bf16[64,8,2432]{2,1,0:T(8,128)(2,1)}), bf16[64,8,2432]{2,1,0:T(8,128)(2,1)S(1)}, u32[]{:S(2)}, u32[]{:S(2)}) %all-to-all-start) | async-done | bytes 2490400 | tf_op jit(solution)/shard_map/all_to_all | solution.py:24
  48.4 1.1 shard_map.172
  49.5 6.6 %all-to-all-start.1 = ((bf16[64,8,384]{2,1,0:T(8,128)(2,1)}), bf16[64,8,384]{2,1,0:T(8,128)(2,1)S(1)}, u32[]{:S(2)}, u32[]{:S(2)}) async-start(bf16[64,8,384]{2,1,0:T(8,128)(2,1)} %bitcast.124), calls=%async_computation.1 | async-start | bytes 786432 | tf_op jit(solution)/shard_map/all_to_all | solution.py:24
  56.1 1.3 fusion.1.adds_ref
  57.4 9.0 %all-to-all-done.1 = bf16[64,8,384]{2,1,0:T(8,128)(2,1)S(1)} async-done(((bf16[64,8,384]{2,1,0:T(8,128)(2,1)}), bf16[64,8,384]{2,1,0:T(8,128)(2,1)S(1)}, u32[]{:S(2)}, u32[]{:S(2)}) %all-to-all-start.1) | async-done | bytes 393248 | tf_op jit(solution)/shard_map/all_to_all | solution.py:24
  66.4 0.9 copy-done.6
  67.4 1.8 shard_map.173
  69.2 6.3 %all-to-all-start.2 = ((bf16[64,8,512]{2,1,0:T(8,128)(2,1)}), bf16[64,8,512]{2,1,0:T(8,128)(2,1)}, u32[]{:S(2)}, u32[]{:S(2)}) async-start(bf16[64,8,512]{2,1,0:T(8,128)(2,1)} %bitcast.129), calls=%async_computation.2 | async-start | bytes 1048576 | tf_op jit(solution)/shard_map/all_to_all | solution.py:24
  75.6 0.6 fusion.39
  76.2 11.1 %all-to-all-done.2 = bf16[64,8,512]{2,1,0:T(8,128)(2,1)} async-done(((bf16[64,8,512]{2,1,0:T(8,128)(2,1)}), bf16[64,8,512]{2,1,0:T(8,128)(2,1)}, u32[]{:S(2)}, u32[]{:S(2)}) %all-to-all-start.2) | async-done | bytes 524320 | tf_op jit(solution)/shard_map/all_to_all | solution.py:24
  87.3 1.2 copy-done.2
  88.5 2.1 shard_map.174
  90.7 0.6 pad_clamp_fusion.2
  91.2 0.9 collective-permute-done
  92.1 0.9 pad_maximum_fusion
  93.0 1.4 gather_fusion
  94.5 1.6 bitcast_reduce_fusion
  96.2 0.2 collective-permute-start.1
  96.4 0.6 compare_select_fusion.3
  97.0 0.6 collective-permute-done.1
  97.6 0.2 fusion.14
  97.8 0.7 multiply_convert_fusion
  98.5 0.2 collective-permute-start.2
  98.7 0.5 compare_select_fusion.4
  99.3 0.7 eq.46
  100.1 1.2 fusion.5
  101.3 0.5 convolution_bitcast_fusion
  101.8 0.4 collective-permute-start.3
  102.3 1.4 gather_fusion.2
  103.7 1.0 fusion.17
  104.8 0.8 gather_fusion.1
  105.7 1.2 maximum_bitcast_fusion
  107.0 22.4 %all_to_all.52 = bf16[64,8,1024]{2,1,0:T(8,128)(2,1)S(1)} all-to-all(bf16[64,8,1024]{2,1,0:T(8,128)(2,1)S(1)} %maximum_bitcast_fusion), channel_id=1, replica_groups=mesh['table'=64,'rep'=4] {'table'}, dimensions={0} | all-to-all | bytes 2097152 | tf_op jit(solution)/shard_map/all_to_all | solution.py:24
  129.4 2.6 %shard_map.175 = (bf16[512,384]{1,0:T(8,128)(2,1)}, f32[512,512]{1,0:T(8,128)}, bf16[256,512]{1,0:T(8,128)(2,1)}, bf16[256,128]{1,0:T(8,128)(2,1)}, f32[8,128]{1,0:T(8,128)}, /*index=5*/f32[8,128]{1,0:T(8,128)}) custom-call(bf16[512,1024]{1,0:T(8,128)(2,1)S(1)} %bitcast.104, bf16[512,128]{1,0:T(8,128)(2,1)S(1)} %copy-done.10, ...), custom_call_target="tpu_custom_call" | custom-call | tf_op jit(solution)/shard_map/pallas_call | solution.py:68
  132.0 5.8 %all-to-all-start.4 = ((bf16[64,8,384]{2,1,0:T(8,128)(2,1)}), bf16[64,8,384]{2,1,0:T(8,128)(2,1)S(1)}, u32[]{:S(2)}, u32[]{:S(2)}) async-start(bf16[64,8,384]{2,1,0:T(8,128)(2,1)} %bitcast.130), calls=%async_computation.4 | async-start | bytes 786432 | tf_op jit(solution)/shard_map/all_to_all | solution.py:24
  138.0 0.1 broadcast_in_dim_reshape.11.index_ref
  138.1 10.2 %all-to-all-done.4 = bf16[64,8,384]{2,1,0:T(8,128)(2,1)S(1)} async-done(((bf16[64,8,384]{2,1,0:T(8,128)(2,1)}), bf16[64,8,384]{2,1,0:T(8,128)(2,1)S(1)}, u32[]{:S(2)}, u32[]{:S(2)}) %all-to-all-start.4) | async-done | bytes 393248 | tf_op jit(solution)/shard_map/all_to_all | solution.py:24
  148.3 0.7 copy-done.15
  149.0 1.1 shard_map.176
  150.2 17.5 %all_to_all.53 = bf16[64,8,512]{2,1,0:T(8,128)(2,1)S(1)} all-to-all(bf16[64,8,512]{2,1,0:T(8,128)(2,1)} %bitcast.120), channel_id=1, replica_groups=mesh['table'=64,'rep'=4] {'table'}, dimensions={0} | all-to-all | bytes 1048576 | tf_op jit(solution)/shard_map/all_to_all | solution.py:24
  167.6 1.4 shard_map.177
  169.0 28.4 %all_to_all.54 = bf16[4,368,256]{2,1,0:T(8,128)(2,1)S(1)} all-to-all(bf16[4,368,256]{2,1,0:T(8,128)(2,1)} %bitcast.118), channel_id=1, replica_groups=mesh['table'=64,'rep'=4] {'rep'}, dimensions={0} | all-to-all | bytes 1507328 | tf_op jit(solution)/shard_map/all_to_all | solution.py:365
  197.4 1.0 shard_map.178
  198.3 3.5 %all-to-all-start.7 = ((bf16[4,368,256]{2,1,0:T(8,128)(2,1)}), bf16[4,368,256]{2,1,0:T(8,128)(2,1)S(1)}, u32[]{:S(2)}, u32[]{:S(2)}) async-start(bf16[4,368,256]{2,1,0:T(8,128)(2,1)} %bitcast.117), calls=%async_computation.7 | async-start | bytes 1507328 | tf_op jit(solution)/shard_map/all_to_all | solution.py:367
  201.9 1.1 fusion.4
  203.0 18.6 %all-to-all-done.7 = bf16[4,368,256]{2,1,0:T(8,128)(2,1)S(1)} async-done(((bf16[4,368,256]{2,1,0:T(8,128)(2,1)}), bf16[4,368,256]{2,1,0:T(8,128)(2,1)S(1)}, u32[]{:S(2)}, u32[]{:S(2)}) %all-to-all-start.7) | async-done | bytes 753696 | tf_op jit(solution)/shard_map/all_to_all | solution.py:367
  221.6 1.2 shard_map.179
  222.8 1.3 slice.56
  224.1 0.8 slice.57
  224.9 0.7 reshape.256
  (90 shorter events, 0.8 us)
Async XLA Ops:
  0.6 1.0 copy-start
  1.7 0.9 copy-start.4
  2.6 0.9 copy-start.11
  3.5 0.8 copy-start.12
  6.3 9.6 %copy-start.28 = (s32[256]{0:T(256)S(1)}, s32[256]{0:T(256)}, u32[]{:S(2)}) copy-start(s32[256]{0:T(256)} %param.13) | copy-start | bytes 3076
  6.3 9.6 %copy-start.29 = (s32[256]{0:T(256)S(1)}, s32[256]{0:T(256)}, u32[]{:S(2)}) copy-start(s32[256]{0:T(256)} %param.17) | copy-start | bytes 3076
  6.3 11.0 %copy-start.30 = (s32[128]{0:T(128)S(1)}, s32[128]{0:T(128)}, u32[]{:S(2)}) copy-start(s32[128]{0:T(128)} %param.19) | copy-start | bytes 1540
  6.4 42.0 %all-to-all-start = ((bf16[64,8,2432]{2,1,0:T(8,128)(2,1)}), bf16[64,8,2432]{2,1,0:T(8,128)(2,1)S(1)}, u32[]{:S(2)}, u32[]{:S(2)}) async-start(bf16[64,8,2432]{2,1,0:T(8,128)(2,1)} %bitcast.116), calls=%async_computation | async-start | bytes 4980736 | tf_op jit(solution)/shard_map/all_to_all | solution.py:24
  16.7 31.7 %copy-start.23 = (s32[256]{0:T(256)}, s32[256]{0:T(256)S(1)}, u32[]{:S(2)}) copy-start(s32[256]{0:T(256)S(1)} %get-tuple-element.42) | copy-start | bytes 3076
  48.4 18.1 %copy-start.1 = (bf16[512,512]{1,0:T(8,128)(2,1)S(1)}, bf16[512,512]{1,0:T(8,128)(2,1)}, u32[]{:S(2)}) copy-start(bf16[512,512]{1,0:T(8,128)(2,1)} %pooled_ref.7) | copy-start | bytes 1572868
  48.4 18.1 %copy-start.16 = (f32[512]{0:T(512)S(1)}, f32[512]{0:T(512)}, u32[]{:S(2)}) copy-start(f32[512]{0:T(512)} %param.16) | copy-start | bytes 6148
  49.5 26.1 %copy-start.22 = (f32[3,4096]{1,0:T(4,128)S(1)}, f32[3,4096]{1,0:T(4,128)}, u32[]{:S(2)}) copy-start(f32[3,4096]{1,0:T(4,128)} %param.21) | copy-start | bytes 147460
  49.5 16.9 %all-to-all-start.1 = ((bf16[64,8,384]{2,1,0:T(8,128)(2,1)}), bf16[64,8,384]{2,1,0:T(8,128)(2,1)S(1)}, u32[]{:S(2)}, u32[]{:S(2)}) async-start(bf16[64,8,384]{2,1,0:T(8,128)(2,1)} %bitcast.124), calls=%async_computation.1 | async-start | bytes 786432 | tf_op jit(solution)/shard_map/all_to_all | solution.py:24
  66.4 1.0 copy-start.6
  69.2 18.1 %all-to-all-start.2 = ((bf16[64,8,512]{2,1,0:T(8,128)(2,1)}), bf16[64,8,512]{2,1,0:T(8,128)(2,1)}, u32[]{:S(2)}, u32[]{:S(2)}) async-start(bf16[64,8,512]{2,1,0:T(8,128)(2,1)} %bitcast.129), calls=%async_computation.2 | async-start | bytes 1048576 | tf_op jit(solution)/shard_map/all_to_all | solution.py:24
  87.3 1.2 copy-start.2
  90.7 1.5 collective-permute-start
  94.4 2.0 copy-start.24
  94.4 3.2 %copy-start.20 = (f32[1,4096]{1,0:T(1,128)S(1)}, f32[1,4096]{1,0:T(1,128)}, u32[]{:S(2)}) copy-start(f32[1,4096]{1,0:T(1,128)} %get-tuple-element.49) | copy-start | bytes 49156
  94.4 3.2 %copy-start.21 = (f32[1,4096]{1,0:T(1,128)S(1)}, f32[1,4096]{1,0:T(1,128)}, u32[]{:S(2)}) copy-start(f32[1,4096]{1,0:T(1,128)} %get-tuple-element.50) | copy-start | bytes 49156
  94.4 3.4 %copy-start.33 = (s32[1,8]{1,0:T(1,128)S(1)}, s32[1,8]{1,0:T(1,128)}, u32[]{:S(2)}) copy-start(s32[1,8]{1,0:T(1,128)} %param.22) | copy-start | bytes 100
  94.4 3.4 %copy-start.34 = (s32[1,8]{1,0:T(1,128)S(1)}, s32[1,8]{1,0:T(1,128)}, u32[]{:S(2)}) copy-start(s32[1,8]{1,0:T(1,128)} %param.23) | copy-start | bytes 100
  94.5 4.2 %copy-start.31 = (s32[128]{0:T(128)S(1)}, s32[128]{0:T(128)}, u32[]{:S(2)}) copy-start(s32[128]{0:T(128)} %param.19) | copy-start | bytes 1540
  96.2 1.4 collective-permute-start.1
  98.5 1.4 collective-permute-start.2
  100.0 1.4 copy-start.27
  100.1 2.2 copy-start.32
  100.1 2.2 copy-start.26
  100.1 2.2 copy-start.17
  101.3 3.4 %copy-start.19 = (bf16[8,32,1,128]{3,1,0,2:T(8,128)(2,1)S(1)}, bf16[8,32,1,128]{3,1,0,2:T(8,128)(2,1)}, u32[]{:S(2)}) copy-start(bf16[8,32,1,128]{3,1,0,2:T(8,128)(2,1)} %get-tuple-element.52) | copy-start | bytes 196612
  101.8 1.9 collective-permute-start.3
  105.7 23.7 %copy-start.3 = (f32[512,512]{1,0:T(8,128)S(1)}, f32[512,512]{1,0:T(8,128)}, u32[]{:S(2)}) copy-start(f32[512,512]{1,0:T(8,128)} %get-tuple-element.29.factor_ref) | copy-start | bytes 3145732
  105.7 23.7 %copy-start.7 = (bf16[256,512]{1,0:T(8,128)(2,1)S(1)}, bf16[256,512]{1,0:T(8,128)(2,1)}, u32[]{:S(2)}) copy-start(bf16[256,512]{1,0:T(8,128)(2,1)} %u_ref.3) | copy-start | bytes 786436
  105.7 23.7 %copy-start.8 = (bf16[512,512]{1,0:T(8,128)(2,1)S(1)}, bf16[512,512]{1,0:T(8,128)(2,1)}, u32[]{:S(2)}) copy-start(bf16[512,512]{1,0:T(8,128)(2,1)} %get-tuple-element.28.lifted_ref) | copy-start | bytes 1572868
  105.7 23.7 %copy-start.10 = (bf16[512,128]{1,0:T(8,128)(2,1)S(1)}, bf16[512,128]{1,0:T(8,128)(2,1)}, u32[]{:S(2)}) copy-start(bf16[512,128]{1,0:T(8,128)(2,1)} %get-tuple-element.27.weight_ref) | copy-start | bytes 393220
  129.4 8.5 %copy-start.25 = (s32[256]{0:T(256)S(1)}, s32[256]{0:T(256)}, u32[]{:S(2)}) copy-start(s32[256]{0:T(256)} %get-tuple-element.41) | copy-start | bytes 3076
  132.0 35.6 %copy-start.9 = (bf16[256,512]{1,0:T(8,128)(2,1)S(1)}, bf16[256,512]{1,0:T(8,128)(2,1)}, u32[]{:S(2)}) copy-start(bf16[256,512]{1,0:T(8,128)(2,1)} %get-tuple-element.33.up_ref) | copy-start | bytes 786436
  132.0 35.6 %copy-start.13 = (bf16[256,128]{1,0:T(8,128)(2,1)S(1)}, bf16[256,128]{1,0:T(8,128)(2,1)}, u32[]{:S(2)}) copy-start(bf16[256,128]{1,0:T(8,128)(2,1)} %get-tuple-element.34.two_ref) | copy-start | bytes 196612
  132.0 35.6 %copy-start.14 = (f32[8,128]{1,0:T(8,128)S(1)}, f32[8,128]{1,0:T(8,128)}, u32[]{:S(2)}) copy-start(f32[8,128]{1,0:T(8,128)} %get-tuple-element.35.bias_ref) | copy-start | bytes 12292
  132.0 16.3 %all-to-all-start.4 = ((bf16[64,8,384]{2,1,0:T(8,128)(2,1)}), bf16[64,8,384]{2,1,0:T(8,128)(2,1)S(1)}, u32[]{:S(2)}, u32[]{:S(2)}) async-start(bf16[64,8,384]{2,1,0:T(8,128)(2,1)} %bitcast.130), calls=%async_computation.4 | async-start | bytes 786432 | tf_op jit(solution)/shard_map/all_to_all | solution.py:24
  148.3 0.7 copy-start.15
  169.0 32.9 %copy-start.5 = (bf16[512,256]{1,0:T(8,128)(2,1)S(1)}, bf16[512,256]{1,0:T(8,128)(2,1)}, u32[]{:S(2)}) copy-start(bf16[512,256]{1,0:T(8,128)(2,1)} %v_ref.1) | copy-start | bytes 786436
  169.0 32.9 %copy-start.18 = (f32[512,512]{1,0:T(8,128)S(1)}, f32[512,512]{1,0:T(8,128)}, u32[]{:S(2)}) copy-start(f32[512,512]{1,0:T(8,128)} %get-tuple-element.30) | copy-start | bytes 3145732
  198.3 23.3 %all-to-all-start.7 = ((bf16[4,368,256]{2,1,0:T(8,128)(2,1)}), bf16[4,368,256]{2,1,0:T(8,128)(2,1)S(1)}, u32[]{:S(2)}, u32[]{:S(2)}) async-start(bf16[4,368,256]{2,1,0:T(8,128)(2,1)} %bitcast.117), calls=%async_computation.7 | async-start | bytes 1507328 | tf_op jit(solution)/shard_map/all_to_all | solution.py:367

commit v4 on v3

--- a/solution.py
+++ b/solution.py
@@ -149,6 +149,25 @@
 
 def contract(left, right, at):
     return lax.dot_general(left, right, (((at,), (at,)), ((), ())), preferred_element_type=F32)
+
+
+def factors_kernel(
+    own_ref, far_ref, preact_ref, adds_ref, picks_ref, hidden_ref, two_ref, terms_ref, out_ref
+):
+    grad_one = ((own_ref[...] + far_ref[...]) * silu_slope(preact_ref[...])).astype(BF)
+    for q in range(4):
+        out_ref[:, q * E : (q + 1) * E] = contract(adds_ref[q], grad_one, 0).astype(BF)
+    hidden = hidden_ref[...]
+    for e in range(2):
+        out_ref[:, (4 + e) * E : (5 + e) * E] = contract(picks_ref[e], hidden, 0).astype(BF)
+    order = one_hot_rows((512, 256), lambda row: (row >> 4) * 8 + (row & 7))
+    out_ref[:, 6 * E : 7 * E] = move_rows(order, two_ref[...])
+    row = lax.broadcasted_iota(jnp.int32, (512, E), 0)
+    out_ref[:, 7 * E :] = jnp.where(
+        ((row >> 3) & 1) == 0,
+        jnp.dot(order, grad_one, preferred_element_type=F32),
+        jnp.dot(order, terms_ref[...], preferred_element_type=F32),
+    ).astype(BF)
 
 
 def owner_kernel(
@@ -284,10 +303,15 @@
     hidden_of_slot = jnp.sum(
         jnp.where(reads, jnp.arange(tables, dtype=jnp.int32)[:, None] // K1, 0), axis=0
     )
-    out_row = lax.broadcasted_iota(jnp.int32, (4, HB * 8, NT * 8), 1)
-    in_row = lax.broadcasted_iota(jnp.int32, (4, HB * 8, NT * 8), 2)
-    wanted = jnp.repeat(hidden_of_slot.reshape(NT, 4).T, 8, axis=1)[:, None, :]
-    adds = ((wanted == out_row // 8) & (out_row % 8 == in_row % 8)).astype(BF)
+    def spread(blocks):
+        shape = (blocks.shape[1], HB * 8, NT * 8)
+        out_row = lax.broadcasted_iota(jnp.int32, shape, 1)
+        in_row = lax.broadcasted_iota(jnp.int32, shape, 2)
+        wanted = jnp.repeat(blocks.T, 8, axis=1)[:, None, :]
+        return ((wanted == out_row // 8) & (out_row % 8 == in_row % 8)).astype(BF)
+
+    adds = spread(hidden_of_slot.reshape(NT, 4))
+    picks = spread(block_index2.reshape(NT, 2))
 
     pair_two = weight2.reshape(2, 16, 8, E).transpose(0, 2, 1, 3).reshape(16, 16 * E)
     (sent,) = call(
@@ -309,35 +333,43 @@
     preact_one, hidden_one = hidden_first(
         got.reshape(512, 512), adds, top_vectors[0].reshape(HB, E)
     )
-    preact_one = preact_one.reshape(HB, 8, E).transpose(1, 0, 2)
-    hidden_one = hidden_one.reshape(HB, 8, E).transpose(1, 0, 2)
-    hidden_both = jnp.concatenate([hidden_one, from_sibling(hidden_one)], axis=0)
-    picked_both = hidden_both[:, half_index]
-    terms_two = jnp.einsum("bnc,ncd->bnd", picked_both, half_two, preferred_element_type=F32)
-    half_sum = terms_two.reshape(16, HB, 2, E).sum(axis=2)
-    preact_two = half_sum[:8] + from_sibling(half_sum[8:]) + top_vectors[1].reshape(-1, E)
-    hidden_two = jax.nn.silu(preact_two).astype(BF)
-    last_weight = top_vectors[2].reshape(-1, E)
-    logit = jnp.sum(hidden_two.astype(F32) * last_weight, axis=(1, 2))
+    def with_sibling(rows):
+        return jnp.concatenate(
+            [rows.reshape(HB, 8, E), from_sibling(rows).reshape(HB, 8, E)], axis=1
+        )
+
+    picked_both = with_sibling(hidden_one)[half_index]
+    terms_two = jnp.einsum("nbc,ncd->nbd", picked_both, half_two, preferred_element_type=F32)
+    half_sum = terms_two.reshape(HB, 2, 16, E).sum(axis=1)
+    preact_two = half_sum[:, :8] + from_sibling(half_sum[:, 8:])
+    preact_two = preact_two + top_vectors[1].reshape(HB, 1, E)
+    hidden_two = jax.nn.silu(preact_two).astype(BF).astype(F32)
+    last_weight = top_vectors[2].reshape(HB, 1, E)
+    logit = jnp.sum(hidden_two * last_weight, axis=(0, 2))
     sample_weight = importance.reshape(-1).astype(F32) / 8.0
-    targets = labels.reshape(-1).astype(F32)
-    grad_logit = sample_weight * (jax.nn.sigmoid(logit) - targets)
-    grad_two = (grad_logit[:, None, None] * last_weight * silu_slope(preact_two)).astype(BF)
-    last_terms = (hidden_two.astype(F32) * grad_logit[:, None, None]).astype(BF)
-    grad_both = jnp.concatenate([grad_two, from_sibling(grad_two)], axis=0)
-    spread_two = jnp.repeat(grad_both, 2, axis=1)
-    back_two = jnp.einsum("bnd,ncd->bnc", spread_two, half_two, preferred_element_type=F32)
-    onehot_two = (half_index[:, None] == jnp.arange(HB, dtype=jnp.int32)[None, :]).astype(F32)
-    half_into = jnp.einsum("bnc,nj->bjc", back_two, onehot_two, precision=lax.Precision.HIGHEST)
-    into_one = half_into[:8] + from_sibling(half_into[8:])
-    grad_one = (into_one * silu_slope(preact_one)).astype(BF)
-
-    spread_one = grad_one[:, hidden_of_slot].reshape(8, NT, 4 * E)
-    picked_pair = hidden_one[:, block_index2].reshape(8, NT, 2 * E)
-    both = jnp.repeat(grad_two, 2, axis=1)
-    third = jnp.stack([grad_one, last_terms], axis=2).reshape(8, NT, E)
-    sent = jnp.concatenate([spread_one, picked_pair, both, third], axis=2).transpose(1, 0, 2)
-    got = exchange(sent).reshape(512, 8 * E)
+    grad_logit = sample_weight * (jax.nn.sigmoid(logit) - labels.reshape(-1).astype(F32))
+    grad_logit = grad_logit[None, :, None]
+    grad_two = (grad_logit * last_weight * silu_slope(preact_two)).astype(BF)
+    grad_two = grad_two.reshape(HB * 8, E)
+    last_terms = (hidden_two * grad_logit).astype(BF).reshape(HB * 8, E)
+    spread_two = jnp.repeat(with_sibling(grad_two), 2, axis=0)
+    back_two = jnp.einsum("nbd,ncd->nbc", spread_two, half_two, preferred_element_type=F32)
+    onehot_two = (jnp.arange(HB, dtype=jnp.int32)[:, None] == half_index[None, :]).astype(F32)
+    half_into = jnp.einsum("jn,nbc->jbc", onehot_two, back_two, precision=lax.Precision.HIGHEST)
+
+    (sent,) = call(
+        factors_kernel,
+        [jax.ShapeDtypeStruct((512, 8 * E), BF)],
+        half_into[:, :8].reshape(HB * 8, E),
+        from_sibling(half_into[:, 8:].reshape(HB * 8, E)),
+        preact_one,
+        adds,
+        picks,
+        hidden_one,
+        grad_two,
+        last_terms,
+    )
+    got = exchange(sent.reshape(NT, 8, 8 * E)).reshape(512, 8 * E)
     sent, direct, local_u, local_two, vector_rows, local_bias = call(
         owner_kernel,
         [

time: 227 us -> 235 us (1.035)
  Pallas kernels: 14.3 us -> 19.1 us
  local copies, waits for them, and re-layouts: 16.5 us -> 20.3 us
    pallas_call x7 -> x8, Pallas kernels: 12 us -> 16.8 us  [call(): pl.pallas_call(kernel, grid=(1,), out_shape=[pltpu.HBM(shape.shape, shape...]
    convert_element_type x3 -> x2, other arithmetic: 3 us -> 0.64 us  [spread(): return ((wanted == out_row // 8) & (out_row % 8 == in_row % 8)).astype(BF)]
    unnamed x71 -> x100, local copies, waits for them, and re-layouts: 6.74 us -> 7.16 us
  transfers between devices with their start and end apart: 9 -> 9, of which waited for: 7 -> 8; matrix products, arithmetic and copies ran while one was open for 4% -> 5% of each run, Pallas kernels for 0% -> 0%
where the time goes in v4:
time: 235 us; the launch traced here: 233 us
  waiting for transfers between devices  79.7 us (34%)
  blocking collectives  68.9 us (29%)
  starting transfers between devices  32.9 us (14%)
  local copies, waits for them, and re-layouts  20.3 us (9%)
  Pallas kernels  19.1 us (8%)
  other arithmetic  6.56 us (3%)
  matrix products  4.45 us (2%)
    all_to_all x4, waiting for transfers between devices, exchange(): lax.all_to_all(parts, 'table', split_axis=0, concat_axis=0, tiled=True)  59.1 us
    all_to_all x2, blocking collectives, exchange(): lax.all_to_all(parts, 'table', split_axis=0, concat_axis=0, tiled=True)  40.5 us
    all_to_all x1, blocking collectives, body(): late = lax.all_to_all(late, 'rep', split_axis=0, concat_axis=0, tiled=True)  28.4 us
    all_to_all x4, starting transfers between devices, exchange(): lax.all_to_all(parts, 'table', split_axis=0, concat_axis=0, tiled=True)  28.3 us
    all_to_all x1, waiting for transfers between devices, body(): late = lax.all_to_all(late, 'rep', split_axis=0, concat_axis=0, tiled=True)  18.6 us
    pallas_call x8, Pallas kernels, call(): pl.pallas_call(kernel, grid=(1,), out_shape=[pltpu.HBM(shape.shape, shape...  16.8 us
    unnamed x100, local copies, waits for them, and re-layouts  7.16 us
  transfers between devices with their start and end apart: 9, of which 8 were waited for; matrix products, arithmetic and copies ran while one was open for 5% of the time, Pallas kernels for 0%

profile of v4, /device:TPU:2, one launch (start us, length us, event | category | flops | bytes accessed | tf_op | source)
XLA Modules:
  0.0 233.3 jit_solution(11074039007450171254)
XLA Ops:
  0.6 1.0 copy-done
  1.7 0.9 copy-done.4
  2.6 0.9 copy-done.14
  3.5 0.8 copy-done.15
  4.4 2.0 shard_map.171
  6.4 9.5 %all-to-all-start = ((bf16[64,8,2432]{2,1,0:T(8,128)(2,1)}), bf16[64,8,2432]{2,1,0:T(8,128)(2,1)S(1)}, u32[]{:S(2)}, u32[]{:S(2)}) async-start(bf16[64,8,2432]{2,1,0:T(8,128)(2,1)} %bitcast.82), calls=%async_computation | async-start | bytes 4980736 | tf_op jit(solution)/shard_map/all_to_all | solution.py:24
  15.9 0.2 reshape.222
  16.1 0.7 dynamic-slice_reduce_fusion
  16.9 0.8 fusion.11
  18.0 0.1 eq.69
  18.2 0.1 broadcast_in_dim_reshape.11.index_ref
  18.3 30.0 %all-to-all-done = bf16[64,8,2432]{2,1,0:T(8,128)(2,1)S(1)} async-done(((bf16[64,8,2432]{2,1,0:T(8,128)(2,1)}), bf16[64,8,2432]{2,1,0:T(8,128)(2,1)S(1)}, u32[]{:S(2)}, u32[]{:S(2)}) %all-to-all-start) | async-done | bytes 2490400 | tf_op jit(solution)/shard_map/all_to_all | solution.py:24
  48.4 1.1 shard_map.172
  49.5 6.6 %all-to-all-start.1 = ((bf16[64,8,384]{2,1,0:T(8,128)(2,1)}), bf16[64,8,384]{2,1,0:T(8,128)(2,1)}, u32[]{:S(2)}, u32[]{:S(2)}) async-start(bf16[64,8,384]{2,1,0:T(8,128)(2,1)} %bitcast.87), calls=%async_computation.1 | async-start | bytes 786432 | tf_op jit(solution)/shard_map/all_to_all | solution.py:24
  56.2 0.4 copy-done.39
  56.8 0.4 fusion.1.adds_ref
  57.2 9.2 %all-to-all-done.1 = bf16[64,8,384]{2,1,0:T(8,128)(2,1)} async-done(((bf16[64,8,384]{2,1,0:T(8,128)(2,1)}), bf16[64,8,384]{2,1,0:T(8,128)(2,1)}, u32[]{:S(2)}, u32[]{:S(2)}) %all-to-all-start.1) | async-done | bytes 393248 | tf_op jit(solution)/shard_map/all_to_all | solution.py:24
  66.4 1.0 copy-done.1
  67.4 0.9 copy-done.6
  68.4 2.8 %shard_map.173 = (bf16[512,512]{1,0:T(8,128)(2,1)}, f32[512,512]{1,0:T(8,128)}, bf16[512,512]{1,0:T(8,128)(2,1)}, bf16[512,128]{1,0:T(8,128)(2,1)}) custom-call(bf16[512,384]{1,0:T(8,128)(2,1)} %bitcast.9.got_ref.crossed_ref, bf16[512,512]{1,0:T(8,128)(2,1)S(1)} %copy-done.1, bf16[256,512]{1,0:T(8,128)(2,1)S(1)} %copy-done.6, f32[1,512]{1,0:T(1,128)S(1)} %bitcast.81), custom_call_target="tpu_custom_call" | custom-call | tf_op jit(solution)/shard_map/pallas_call | solution.py:68
  71.2 6.4 %all-to-all-start.2 = ((bf16[64,8,512]{2,1,0:T(8,128)(2,1)}), bf16[64,8,512]{2,1,0:T(8,128)(2,1)}, u32[]{:S(2)}, u32[]{:S(2)}) async-start(bf16[64,8,512]{2,1,0:T(8,128)(2,1)} %bitcast.89), calls=%async_computation.2 | async-start | bytes 1048576 | tf_op jit(solution)/shard_map/all_to_all | solution.py:24
  77.5 0.5 fusion.29
  78.1 1.6 fusion.31
  79.7 9.6 %all-to-all-done.2 = bf16[64,8,512]{2,1,0:T(8,128)(2,1)} async-done(((bf16[64,8,512]{2,1,0:T(8,128)(2,1)}), bf16[64,8,512]{2,1,0:T(8,128)(2,1)}, u32[]{:S(2)}, u32[]{:S(2)}) %all-to-all-start.2) | async-done | bytes 524320 | tf_op jit(solution)/shard_map/all_to_all | solution.py:24
  89.3 2.1 shard_map.174
  91.4 1.2 pad_clamp_fusion
  92.7 0.2 collective-permute-done
  92.9 1.5 pad_maximum_fusion
  94.4 2.4 %gather_fusion = bf16[64,16,128]{2,1,0:T(8,128)(2,1)} fusion(bf16[32,16,128]{2,1,0:T(8,128)(2,1)} %pad_maximum_fusion, s32[1024]{0:T(1024)} %pad_clamp_fusion), kind=kCustom, calls=%fused_computation | custom fusion | bytes 524544 | tf_op jit(solution)/shard_map/gather | solution.py:341
  96.8 1.6 bitcast_reduce_fusion
  98.5 0.4 collective-permute-start.1
  98.8 1.1 collective-permute-done.1
  99.9 0.2 fusion.13
  100.1 0.8 fusion.16
  100.9 0.3 collective-permute-start.2
  101.2 0.6 eq.63
  101.8 1.4 reshape.245
  103.2 0.8 copy.33
  104.0 0.7 broadcast_in_dim.57
  104.7 0.9 eq.73
  105.7 0.9 pad_maximum_fusion.1
  106.7 1.2 fusion.2
  107.9 0.5 fusion.7
  108.5 0.5 collective-permute-start.3
  109.1 0.3 fusion.6.picks_ref
  109.5 0.7 collective-permute-done.3.far_ref
  110.2 2.8 %shard_map.175 = bf16[512,1024]{1,0:T(8,128)(2,1)} custom-call(f32[256,128]{1,0:T(8,128)S(1)} %bitcast.76, f32[256,128]{1,0:T(8,128)S(1)} %collective-permute-done.3.far_ref, f32[256,128]{1,0:T(8,128)S(1)} %copy-done.13, bf16[4,256,512]{2,1,0:T(8,128)(2,1)S(1)} %fusion.1.adds_ref, bf16[2,256,512]{2,1,0:T(8,128)(2,1)S(1)} %fusion.6.picks_ref, ...), custom_call_target="tpu_custom_call" | custom-call | tf_op jit(solution)/shard_map/pallas_call | solution.py:68
  113.0 23.1 %all_to_all.52 = bf16[64,8,1024]{2,1,0:T(8,128)(2,1)S(1)} all-to-all(bf16[64,8,1024]{2,1,0:T(8,128)(2,1)} %bitcast.83), channel_id=1, replica_groups=mesh['table'=64,'rep'=4] {'table'}, dimensions={0} | all-to-all | bytes 2097152 | tf_op jit(solution)/shard_map/all_to_all | solution.py:24
  136.1 3.6 %shard_map.176 = (bf16[512,384]{1,0:T(8,128)(2,1)}, f32[512,512]{1,0:T(8,128)}, bf16[256,512]{1,0:T(8,128)(2,1)}, bf16[256,128]{1,0:T(8,128)(2,1)}, f32[8,128]{1,0:T(8,128)}, /*index=5*/f32[8,128]{1,0:T(8,128)}) custom-call(bf16[512,1024]{1,0:T(8,128)(2,1)S(1)} %bitcast.70, bf16[512,128]{1,0:T(8,128)(2,1)S(1)} %copy-done.12, bf16[512,512]{1,0:T(8,128)(2,1)S(1)} %copy-done.8, ...), custom_call_target="tpu_custom_call" | custom-call | tf_op jit(solution)/shard_map/pallas_call | solution.py:68
  139.7 5.8 %all-to-all-start.4 = ((bf16[64,8,384]{2,1,0:T(8,128)(2,1)}), bf16[64,8,384]{2,1,0:T(8,128)(2,1)S(1)}, u32[]{:S(2)}, u32[]{:S(2)}) async-start(bf16[64,8,384]{2,1,0:T(8,128)(2,1)} %bitcast.90), calls=%async_computation.4 | async-start | bytes 786432 | tf_op jit(solution)/shard_map/all_to_all | solution.py:24
  145.8 10.2 %all-to-all-done.4 = bf16[64,8,384]{2,1,0:T(8,128)(2,1)S(1)} async-done(((bf16[64,8,384]{2,1,0:T(8,128)(2,1)}), bf16[64,8,384]{2,1,0:T(8,128)(2,1)S(1)}, u32[]{:S(2)}, u32[]{:S(2)}) %all-to-all-start.4) | async-done | bytes 393248 | tf_op jit(solution)/shard_map/all_to_all | solution.py:24
  156.0 0.7 copy-done.18
  156.7 1.1 shard_map.177
  157.9 17.5 %all_to_all.53 = bf16[64,8,512]{2,1,0:T(8,128)(2,1)S(1)} all-to-all(bf16[64,8,512]{2,1,0:T(8,128)(2,1)} %bitcast.86), channel_id=1, replica_groups=mesh['table'=64,'rep'=4] {'table'}, dimensions={0} | all-to-all | bytes 1048576 | tf_op jit(solution)/shard_map/all_to_all | solution.py:24
  175.3 1.4 shard_map.178
  176.7 28.4 %all_to_all.54 = bf16[4,368,256]{2,1,0:T(8,128)(2,1)S(1)} all-to-all(bf16[4,368,256]{2,1,0:T(8,128)(2,1)} %bitcast.85), channel_id=1, replica_groups=mesh['table'=64,'rep'=4] {'rep'}, dimensions={0} | all-to-all | bytes 1507328 | tf_op jit(solution)/shard_map/all_to_all | solution.py:397
  205.1 1.0 shard_map.179
  206.1 3.5 %all-to-all-start.7 = ((bf16[4,368,256]{2,1,0:T(8,128)(2,1)}), bf16[4,368,256]{2,1,0:T(8,128)(2,1)S(1)}, u32[]{:S(2)}, u32[]{:S(2)}) async-start(bf16[4,368,256]{2,1,0:T(8,128)(2,1)} %bitcast.84), calls=%async_computation.7 | async-start | bytes 1507328 | tf_op jit(solution)/shard_map/all_to_all | solution.py:399
  209.6 1.1 fusion.4
  210.7 18.6 %all-to-all-done.7 = bf16[4,368,256]{2,1,0:T(8,128)(2,1)S(1)} async-done(((bf16[4,368,256]{2,1,0:T(8,128)(2,1)}), bf16[4,368,256]{2,1,0:T(8,128)(2,1)S(1)}, u32[]{:S(2)}, u32[]{:S(2)}) %all-to-all-start.7) | async-done | bytes 753696 | tf_op jit(solution)/shard_map/all_to_all | solution.py:399
  229.4 1.2 shard_map.180
  230.5 0.8 slice.53
  231.3 1.3 slice.52
  232.6 0.7 reshape.256
  (113 shorter events, 1.3 us)
Async XLA Ops:
  0.6 1.0 copy-start
  1.7 0.9 copy-start.4
  2.6 0.9 copy-start.14
  3.5 0.8 copy-start.15
  6.3 9.5 %copy-start.38 = (s32[128]{0:T(128)S(1)}, s32[128]{0:T(128)}, u32[]{:S(2)}) copy-start(s32[128]{0:T(128)} %param.19) | copy-start | bytes 1540
  6.3 10.5 %copy-start.46 = (s32[256]{0:T(256)S(1)}, s32[256]{0:T(256)}, u32[]{:S(2)}) copy-start(s32[256]{0:T(256)} %param.13) | copy-start | bytes 3076
  6.3 10.5 %copy-start.47 = (s32[256]{0:T(256)S(1)}, s32[256]{0:T(256)}, u32[]{:S(2)}) copy-start(s32[256]{0:T(256)} %param.17) | copy-start | bytes 3076
  6.4 42.0 %all-to-all-start = ((bf16[64,8,2432]{2,1,0:T(8,128)(2,1)}), bf16[64,8,2432]{2,1,0:T(8,128)(2,1)S(1)}, u32[]{:S(2)}, u32[]{:S(2)}) async-start(bf16[64,8,2432]{2,1,0:T(8,128)(2,1)} %bitcast.82), calls=%async_computation | async-start | bytes 4980736 | tf_op jit(solution)/shard_map/all_to_all | solution.py:24
  16.8 1.0 copy-start.21
  48.4 18.0 %copy-start.19 = (f32[512]{0:T(512)S(1)}, f32[512]{0:T(512)}, u32[]{:S(2)}) copy-start(f32[512]{0:T(512)} %param.16) | copy-start | bytes 6148
  49.5 16.9 %all-to-all-start.1 = ((bf16[64,8,384]{2,1,0:T(8,128)(2,1)}), bf16[64,8,384]{2,1,0:T(8,128)(2,1)}, u32[]{:S(2)}, u32[]{:S(2)}) async-start(bf16[64,8,384]{2,1,0:T(8,128)(2,1)} %bitcast.87), calls=%async_computation.1 | async-start | bytes 786432 | tf_op jit(solution)/shard_map/all_to_all | solution.py:24
  56.1 0.6 copy-start.39
  56.1 0.6 copy-start.41
  56.1 0.6 copy-start.43
  56.1 0.6 copy-start.29
  56.1 0.6 copy-start.31
  56.2 0.6 copy-start.33
  56.2 0.6 copy-start.35
  56.2 0.6 copy-start.25
  56.2 0.6 copy-start.27
  66.4 1.0 copy-start.1
  67.4 0.9 copy-start.6
  71.2 18.1 %all-to-all-start.2 = ((bf16[64,8,512]{2,1,0:T(8,128)(2,1)}), bf16[64,8,512]{2,1,0:T(8,128)(2,1)}, u32[]{:S(2)}, u32[]{:S(2)}) async-start(bf16[64,8,512]{2,1,0:T(8,128)(2,1)} %bitcast.89), calls=%async_computation.2 | async-start | bytes 1048576 | tf_op jit(solution)/shard_map/all_to_all | solution.py:24
  91.4 1.5 collective-permute-start
  94.4 6.7 %copy-start.22 = (s32[32,2]{1,0:T(8,128)S(1)}, s32[32,2]{1,0:T(8,128)}, u32[]{:S(2)}) copy-start(s32[32,2]{1,0:T(8,128)} %copy-done.21) | copy-start | bytes 772
  96.8 3.1 %copy-start.23 = (f32[1,4096]{1,0:T(1,128)S(1)}, f32[1,4096]{1,0:T(1,128)}, u32[]{:S(2)}) copy-start(f32[1,4096]{1,0:T(1,128)} %get-tuple-element.49) | copy-start | bytes 49156
  96.8 3.1 %copy-start.24 = (f32[1,4096]{1,0:T(1,128)S(1)}, f32[1,4096]{1,0:T(1,128)}, u32[]{:S(2)}) copy-start(f32[1,4096]{1,0:T(1,128)} %get-tuple-element.50) | copy-start | bytes 49156
  96.8 3.3 %copy-start.48 = (s32[1,8]{1,0:T(1,128)S(1)}, s32[1,8]{1,0:T(1,128)}, u32[]{:S(2)}) copy-start(s32[1,8]{1,0:T(1,128)} %param.22) | copy-start | bytes 100
  96.8 3.3 %copy-start.49 = (s32[1,8]{1,0:T(1,128)S(1)}, s32[1,8]{1,0:T(1,128)}, u32[]{:S(2)}) copy-start(s32[1,8]{1,0:T(1,128)} %param.23) | copy-start | bytes 100
  98.5 1.4 collective-permute-start.1
  100.9 4.8 %collective-permute-start.2 = (bf16[256,128]{1,0:T(8,128)(2,1)}, bf16[256,128]{1,0:T(8,128)(2,1)}, u32[]{:S(2)}, u32[]{:S(2)}) collective-permute-start(bf16[256,128]{1,0:T(8,128)(2,1)} %bitcast.25.two_ref), channel_id=1, source_target_pairs={{0,4},{4,0},{8,12},{12,8},{16,20},{20,16},{24,28},{28,24},{32,36},... | collective-permute-start | bytes 196616 | tf_op jit(solution)/shard_map/ppermute | solution.py:28
  101.8 6.2 %copy-start.45 = (s32[64]{0:T(128)S(1)}, s32[64]{0:T(128)}, u32[]{:S(2)}) copy-start(s32[64]{0:T(128)} %eq.63) | copy-start | bytes 772
  106.6 2.4 %copy-start.26 = (s32[512]{0:T(512)S(1)}, s32[512]{0:T(512)}, u32[]{:S(2)}) copy-start(s32[512]{0:T(512)} %copy-done.25) | copy-start | bytes 6148
  106.6 2.4 %copy-start.28 = (s32[512]{0:T(512)S(1)}, s32[512]{0:T(512)}, u32[]{:S(2)}) copy-start(s32[512]{0:T(512)} %copy-done.27) | copy-start | bytes 6148
  106.6 2.4 %copy-start.30 = (s32[256]{0:T(256)S(1)}, s32[256]{0:T(256)}, u32[]{:S(2)}) copy-start(s32[256]{0:T(256)} %copy-done.29) | copy-start | bytes 3076
  106.6 2.4 %copy-start.32 = (s32[256]{0:T(256)S(1)}, s32[256]{0:T(256)}, u32[]{:S(2)}) copy-start(s32[256]{0:T(256)} %copy-done.31) | copy-start | bytes 3076
  106.6 2.4 %copy-start.34 = (s32[256]{0:T(256)S(1)}, s32[256]{0:T(256)}, u32[]{:S(2)}) copy-start(s32[256]{0:T(256)} %copy-done.33) | copy-start | bytes 3076
  106.7 2.4 %copy-start.36 = (s32[256]{0:T(256)S(1)}, s32[256]{0:T(256)}, u32[]{:S(2)}) copy-start(s32[256]{0:T(256)} %copy-done.35) | copy-start | bytes 3076
  106.7 2.4 %copy-start.40 = (pred[512]{0:T(512)(128)(4,1)S(1)}, pred[512]{0:T(512)(128)(4,1)}, u32[]{:S(2)}) copy-start(pred[512]{0:T(512)(128)(4,1)} %copy-done.39) | copy-start | bytes 1540
  106.7 2.4 %copy-start.42 = (pred[256]{0:T(512)(128)(4,1)S(1)}, pred[256]{0:T(512)(128)(4,1)}, u32[]{:S(2)}) copy-start(pred[256]{0:T(512)(128)(4,1)} %copy-done.41) | copy-start | bytes 772
  106.7 2.4 %copy-start.44 = (pred[256]{0:T(512)(128)(4,1)S(1)}, pred[256]{0:T(512)(128)(4,1)}, u32[]{:S(2)}) copy-start(pred[256]{0:T(512)(128)(4,1)} %copy-done.43) | copy-start | bytes 772
  106.7 3.5 %copy-start.9 = (bf16[256,128]{1,0:T(8,128)(2,1)S(1)}, bf16[256,128]{1,0:T(8,128)(2,1)}, u32[]{:S(2)}) copy-start(bf16[256,128]{1,0:T(8,128)(2,1)} %get-tuple-element.51.terms_ref) | copy-start | bytes 196612
  106.7 3.4 %copy-start.10 = (bf16[256,128]{1,0:T(8,128)(2,1)S(1)}, bf16[256,128]{1,0:T(8,128)(2,1)}, u32[]{:S(2)}) copy-start(bf16[256,128]{1,0:T(8,128)(2,1)} %get-tuple-element.25.hidden_ref) | copy-start | bytes 196612
  106.7 3.4 %copy-start.13 = (f32[256,128]{1,0:T(8,128)S(1)}, f32[256,128]{1,0:T(8,128)}, u32[]{:S(2)}) copy-start(f32[256,128]{1,0:T(8,128)} %get-tuple-element.26.preact_ref) | copy-start | bytes 393220
  108.5 1.6 collective-permute-start.3
  110.2 25.9 %copy-start.2 = (bf16[512,512]{1,0:T(8,128)(2,1)S(1)}, bf16[512,512]{1,0:T(8,128)(2,1)}, u32[]{:S(2)}) copy-start(bf16[512,512]{1,0:T(8,128)(2,1)} %pooled_ref.7) | copy-start | bytes 1572868
  110.2 25.9 %copy-start.3 = (f32[512,512]{1,0:T(8,128)S(1)}, f32[512,512]{1,0:T(8,128)}, u32[]{:S(2)}) copy-start(f32[512,512]{1,0:T(8,128)} %get-tuple-element.29.factor_ref) | copy-start | bytes 3145732
  110.2 25.9 %copy-start.7 = (bf16[256,512]{1,0:T(8,128)(2,1)S(1)}, bf16[256,512]{1,0:T(8,128)(2,1)}, u32[]{:S(2)}) copy-start(bf16[256,512]{1,0:T(8,128)(2,1)} %u_ref.3) | copy-start | bytes 786436
  110.2 25.9 %copy-start.8 = (bf16[512,512]{1,0:T(8,128)(2,1)S(1)}, bf16[512,512]{1,0:T(8,128)(2,1)}, u32[]{:S(2)}) copy-start(bf16[512,512]{1,0:T(8,128)(2,1)} %get-tuple-element.28.lifted_ref) | copy-start | bytes 1572868
  110.2 25.9 %copy-start.12 = (bf16[512,128]{1,0:T(8,128)(2,1)S(1)}, bf16[512,128]{1,0:T(8,128)(2,1)}, u32[]{:S(2)}) copy-start(bf16[512,128]{1,0:T(8,128)(2,1)} %get-tuple-element.27.weight_ref) | copy-start | bytes 393220
  136.1 9.4 %copy-start.37 = (s32[256]{0:T(256)S(1)}, s32[256]{0:T(256)}, u32[]{:S(2)}) copy-start(s32[256]{0:T(256)} %get-tuple-element.41) | copy-start | bytes 3076
  139.7 35.6 %copy-start.11 = (bf16[256,512]{1,0:T(8,128)(2,1)S(1)}, bf16[256,512]{1,0:T(8,128)(2,1)}, u32[]{:S(2)}) copy-start(bf16[256,512]{1,0:T(8,128)(2,1)} %get-tuple-element.33.up_ref) | copy-start | bytes 786436
  139.7 35.6 %copy-start.16 = (bf16[256,128]{1,0:T(8,128)(2,1)S(1)}, bf16[256,128]{1,0:T(8,128)(2,1)}, u32[]{:S(2)}) copy-start(bf16[256,128]{1,0:T(8,128)(2,1)} %get-tuple-element.34.two_ref) | copy-start | bytes 196612
  139.7 35.6 %copy-start.17 = (f32[8,128]{1,0:T(8,128)S(1)}, f32[8,128]{1,0:T(8,128)}, u32[]{:S(2)}) copy-start(f32[8,128]{1,0:T(8,128)} %get-tuple-element.35.bias_ref) | copy-start | bytes 12292
  139.7 16.3 %all-to-all-start.4 = ((bf16[64,8,384]{2,1,0:T(8,128)(2,1)}), bf16[64,8,384]{2,1,0:T(8,128)(2,1)S(1)}, u32[]{:S(2)}, u32[]{:S(2)}) async-start(bf16[64,8,384]{2,1,0:T(8,128)(2,1)} %bitcast.90), calls=%async_computation.4 | async-start | bytes 786432 | tf_op jit(solution)/shard_map/all_to_all | solution.py:24
  156.0 0.7 copy-start.18
  176.7 32.9 %copy-start.5 = (bf16[512,256]{1,0:T(8,128)(2,1)S(1)}, bf16[512,256]{1,0:T(8,128)(2,1)}, u32[]{:S(2)}) copy-start(bf16[512,256]{1,0:T(8,128)(2,1)} %v_ref.1) | copy-start | bytes 786436
  176.7 32.9 %copy-start.20 = (f32[512,512]{1,0:T(8,128)S(1)}, f32[512,512]{1,0:T(8,128)}, u32[]{:S(2)}) copy-start(f32[512,512]{1,0:T(8,128)} %get-tuple-element.30) | copy-start | bytes 3145732
  206.1 23.3 %all-to-all-start.7 = ((bf16[4,368,256]{2,1,0:T(8,128)(2,1)}), bf16[4,368,256]{2,1,0:T(8,128)(2,1)S(1)}, u32[]{:S(2)}, u32[]{:S(2)}) async-start(bf16[4,368,256]{2,1,0:T(8,128)(2,1)} %bitcast.84), calls=%async_computation.7 | async-start | bytes 1507328 | tf_op jit(solution)/shard_map/all_to_all | solution.py:399

commit v5 on v3

--- a/solution.py
+++ b/solution.py
@@ -107,14 +107,11 @@
     )
 
 
-def start_kernel(pooled_ref, v_ref, weight_ref, pair_ref, out_ref):
+def start_kernel(pooled_ref, v_ref, weight_ref, out_ref):
     out_ref[:, :256] = jnp.dot(
         pooled_ref[...], v_ref[...], preferred_element_type=F32
     ).astype(BF)
     out_ref[:, 256:384] = move_rows(one_hot_rows((512, 512), to_pieces), weight_ref[...])
-    pair = pair_ref[...]
-    for i in range(32):
-        out_ref[16 * i : 16 * i + 16, 384:] = pair
 
 
 def regroup_kernel(got_ref, index_ref, extra_ref, out_ref):
@@ -272,7 +269,7 @@
     tables = table_slot.shape[0]
     contract_last = (((1,), (1,)), ((), ()))
     core = lax.axis_index("table") % 2
-    half_index = lax.dynamic_index_in_dim(block_index2.reshape(HB, 2, 2), core, 2, keepdims=False)
+    half_index = lax.dynamic_index_in_dim(block_index2.reshape(HB, 2, 2), core, 1, keepdims=False)
     half_index = half_index.reshape(-1)
 
     reads = block_index1[:, None] == table_slot[None, :]
@@ -289,18 +286,23 @@
     wanted = jnp.repeat(hidden_of_slot.reshape(NT, 4).T, 8, axis=1)[:, None, :]
     adds = ((wanted == out_row // 8) & (out_row % 8 == in_row % 8)).astype(BF)
 
-    pair_two = weight2.reshape(2, 16, 8, E).transpose(0, 2, 1, 3).reshape(16, 16 * E)
     (sent,) = call(
         start_kernel,
-        [jax.ShapeDtypeStruct((512, 2432), BF)],
+        [jax.ShapeDtypeStruct((512, 384), BF)],
         pooled,
         cross_v,
         weight1.reshape(512, E),
-        pair_two,
-    )
-    got = exchange(sent.reshape(NT, 8, 2432))
-    half_two = got[:, :, 384:].reshape(NT, 8, 16, E).transpose(0, 2, 1, 3).reshape(NT, E, E)
-    sent = regroup(got.reshape(512, 2432), block_of_slot)
+    )
+    got = exchange(sent.reshape(NT, 8, 384))
+    half_two = lax.all_to_all(
+        jnp.broadcast_to(weight2[None], (HB, 2, E, E)),
+        "table",
+        split_axis=0,
+        concat_axis=0,
+        tiled=True,
+        axis_index_groups=[list(range(at, NT, 2)) for at in range(2)],
+    ).reshape(NT, E, E)
+    sent = regroup(got.reshape(512, 384), block_of_slot)
     arrived = exchange(sent.reshape(NT, 8, 384)).reshape(512, 384)
     lifted, factor, terms, weight_slot = lift(
         arrived, pooled, cross_u, cross_bias.reshape(1, 512)

time: 227 us -> 231 us (1.018)
  blocking collectives: 68.3 us -> 102 us
  waiting for transfers between devices: 80.6 us -> 66.4 us
  starting transfers between devices: 32.6 us -> 25.3 us
  other arithmetic: 7.8 us -> 2 us
  local copies, waits for them, and re-layouts: 16.5 us -> 13.1 us
    all_to_all x4 -> x2, waiting for transfers between devices: 60.4 us -> 20.2 us  [exchange(): lax.all_to_all(parts, 'table', split_axis=0, concat_axis=0, tiled=True)]
    all_to_all x2 -> x4, blocking collectives: 39.9 us -> 74 us  [exchange(): lax.all_to_all(parts, 'table', split_axis=0, concat_axis=0, tiled=True)]
    all_to_all x0 -> x1, waiting for transfers between devices: none -> 23.4 us  [body(): lax.all_to_all(jnp.broadcast_to(weight2[None], (HB, 2, E, E)), 'table', s...]
    all_to_all x4 -> x2, starting transfers between devices: 28.2 us -> 15.2 us  [exchange(): lax.all_to_all(parts, 'table', split_axis=0, concat_axis=0, tiled=True)]
    all_to_all x0 -> x1, starting transfers between devices: none -> 6.01 us  [body(): lax.all_to_all(jnp.broadcast_to(weight2[None], (HB, 2, E, E)), 'table', s...]
    unnamed x71 -> x49, local copies, waits for them, and re-layouts: 6.74 us -> 3.7 us
    ppermute x4, waiting for transfers between devices: 1.51 us -> 4.22 us  [from_sibling(): return lax.ppermute(value, 'table', [(i, i ^ 1) for i in range(NT)])]
  transfers between devices with their start and end apart: 9 -> 8, of which waited for: 7 -> 8; matrix products, arithmetic and copies ran while one was open for 4% -> 3% of each run, Pallas kernels for 0% -> 0%
where the time goes in v5:
time: 231 us; the launch traced here: 229 us
  blocking collectives  102 us (44%)
  waiting for transfers between devices  66.4 us (29%)
  starting transfers between devices  25.3 us (11%)
  local copies, waits for them, and re-layouts  13.1 us (6%)
  Pallas kernels  12.5 us (5%)
  matrix products  6.68 us (3%)
    all_to_all x4, blocking collectives, exchange(): lax.all_to_all(parts, 'table', split_axis=0, concat_axis=0, tiled=True)  74 us
    all_to_all x1, blocking collectives, body(): late = lax.all_to_all(late, 'rep', split_axis=0, concat_axis=0, tiled=True)  28.4 us
    all_to_all x1, waiting for transfers between devices, body(): lax.all_to_all(jnp.broadcast_to(weight2[None], (HB, 2, E, E)), 'table', s...  23.4 us
    all_to_all x2, waiting for transfers between devices, exchange(): lax.all_to_all(parts, 'table', split_axis=0, concat_axis=0, tiled=True)  20.2 us
    all_to_all x1, waiting for transfers between devices, body(): late = lax.all_to_all(late, 'rep', split_axis=0, concat_axis=0, tiled=True)  18.6 us
    all_to_all x2, starting transfers between devices, exchange(): lax.all_to_all(parts, 'table', split_axis=0, concat_axis=0, tiled=True)  15.2 us
    pallas_call x7, Pallas kernels, call(): pl.pallas_call(kernel, grid=(1,), out_shape=[pltpu.HBM(shape.shape, shape...  10.2 us
    all_to_all x1, starting transfers between devices, body(): lax.all_to_all(jnp.broadcast_to(weight2[None], (HB, 2, E, E)), 'table', s...  6.01 us
  transfers between devices with their start and end apart: 8, of which 8 were waited for; matrix products, arithmetic and copies ran while one was open for 3% of the time, Pallas kernels for 0%

profile of v5, /device:TPU:2, one launch (start us, length us, event | category | flops | bytes accessed | tf_op | source)
XLA Modules:
  0.0 229.4 jit_solution(13655398015472587060)
XLA Ops:
  0.7 1.0 copy-done
  1.7 0.9 copy-done.3
  2.6 0.9 copy-done.8
  3.6 1.2 shard_map.171
  4.8 9.4 %all-to-all-start = ((bf16[64,8,384]{2,1,0:T(8,128)(2,1)}), bf16[64,8,384]{2,1,0:T(8,128)(2,1)S(1)}, u32[]{:S(2)}, u32[]{:S(2)}) async-start(bf16[64,8,384]{2,1,0:T(8,128)(2,1)} %bitcast.110), calls=%async_computation | async-start | bytes 786432 | tf_op jit(solution)/shard_map/all_to_all | solution.py:24
  14.2 0.2 fusion.6
  14.4 0.1 broadcast_in_dim.64
  14.5 0.1 broadcast_in_dim_reshape.10.index_ref
  14.6 9.9 %all-to-all-done = bf16[64,8,384]{2,1,0:T(8,128)(2,1)S(1)} async-done(((bf16[64,8,384]{2,1,0:T(8,128)(2,1)}), bf16[64,8,384]{2,1,0:T(8,128)(2,1)S(1)}, u32[]{:S(2)}, u32[]{:S(2)}) %all-to-all-start) | async-done | bytes 393248 | tf_op jit(solution)/shard_map/all_to_all | solution.py:24
  24.5 1.1 shard_map.172
  25.6 16.1 %all_to_all.57 = bf16[64,8,384]{2,1,0:T(8,128)(2,1)S(1)} all-to-all(bf16[64,8,384]{2,1,0:T(8,128)(2,1)} %bitcast.111), channel_id=1, replica_groups=mesh['table'=64,'rep'=4] {'table'}, dimensions={0} | all-to-all | bytes 786432 | tf_op jit(solution)/shard_map/all_to_all | solution.py:24
  41.7 1.8 shard_map.173
  43.5 17.5 %all_to_all.58 = bf16[64,8,512]{2,1,0:T(8,128)(2,1)S(1)} all-to-all(bf16[64,8,512]{2,1,0:T(8,128)(2,1)} %bitcast.117), channel_id=1, replica_groups=mesh['table'=64,'rep'=4] {'table'}, dimensions={0} | all-to-all | bytes 1048576 | tf_op jit(solution)/shard_map/all_to_all | solution.py:24
  61.0 1.8 broadcast_in_dim.67
  62.8 6.0 %all-to-all-start.3 = ((bf16[32,2,128,128]{3,2,1,0:T(8,128)(2,1)}), bf16[32,2,128,128]{3,2,1,0:T(8,128)(2,1)}, u32[]{:S(2)}, u32[]{:S(2)}) async-start(bf16[32,2,128,128]{3,2,1,0:T(8,128)(2,1)} %broadcast_in_dim.67), calls=%async_computation.3 | async-start | bytes 4194304 | tf_op jit(solution)/shard_map/all_to_all | solution.py:297
  68.9 0.1 reshape.226
  69.0 0.1 copy.41
  69.0 0.1 broadcast_in_dim.66
  69.2 0.1 eq.53
  69.3 0.2 reshape.217
  69.5 0.5 broadcast.162
  70.0 0.7 fusion.36
  70.7 0.1 reshape.228
  70.8 0.4 fusion.1.adds_ref
  71.3 1.1 shard_map.174
  72.4 1.5 collective-permute-done
  73.8 0.9 pad_maximum_fusion
  74.7 0.6 gather_fusion
  75.4 23.4 %all-to-all-done.3 = bf16[32,2,128,128]{3,2,1,0:T(8,128)(2,1)} async-done(((bf16[32,2,128,128]{3,2,1,0:T(8,128)(2,1)}), bf16[32,2,128,128]{3,2,1,0:T(8,128)(2,1)}, u32[]{:S(2)}, u32[]{:S(2)}) %all-to-all-start.3) | async-done | bytes 2097184 | tf_op jit(solution)/shard_map/all_to_all | solution.py:297
  98.7 2.3 bitcast_reduce_fusion
  101.0 0.1 collective-permute-start.1
  101.2 1.3 collective-permute-done.1
  102.5 0.2 fusion.12
  102.7 0.1 multiply_convert_fusion
  102.8 0.2 collective-permute-start.2
  103.0 0.1 eq.46
  103.1 1.0 collective-permute-done.2
  104.3 2.8 %convolution_bitcast_fusion = f32[16,64,128]{2,0,1:T(8,128)S(1)} fusion(bf16[16,64,128]{2,0,1:T(8,128)(2,1)S(1)} %bitcast.113, bf16[64,128,128]{2,1,0:T(8,128)(2,1)} %bitcast.17), kind=kOutput, calls=%fused_computation.9 | convolution fusion | flops 33554432 | bytes 2883584 | tf_op jit(solution)/shard_map/bnd,ncd->bnc/dot_general | solution.py:331
  107.1 0.5 convolution_bitcast_fusion.1
  107.6 0.2 collective-permute-start.3
  107.9 0.7 gather_fusion.2
  108.6 0.4 collective-permute-done.3
  109.0 0.1 fusion.15
  109.2 0.8 gather_fusion.1
  110.1 0.1 maximum_bitcast_fusion
  110.3 23.0 %all_to_all.59 = bf16[64,8,1024]{2,1,0:T(8,128)(2,1)S(1)} all-to-all(bf16[64,8,1024]{2,1,0:T(8,128)(2,1)S(1)} %maximum_bitcast_fusion), channel_id=1, replica_groups=mesh['table'=64,'rep'=4] {'table'}, dimensions={0} | all-to-all | bytes 2097152 | tf_op jit(solution)/shard_map/all_to_all | solution.py:24
  133.3 2.6 %shard_map.175 = (bf16[512,384]{1,0:T(8,128)(2,1)}, f32[512,512]{1,0:T(8,128)}, bf16[256,512]{1,0:T(8,128)(2,1)}, bf16[256,128]{1,0:T(8,128)(2,1)}, f32[8,128]{1,0:T(8,128)}, /*index=5*/f32[8,128]{1,0:T(8,128)}) custom-call(bf16[512,1024]{1,0:T(8,128)(2,1)S(1)} %bitcast.90, bf16[512,128]{1,0:T(8,128)(2,1)S(1)} %copy-done.9, bf16[512,512]{1,0:T(8,128)(2,1)S(1)} %copy-done.6, ...), custom_call_target="tpu_custom_call" | custom-call | tf_op jit(solution)/shard_map/pallas_call | solution.py:68
  135.9 5.8 %all-to-all-start.5 = ((bf16[64,8,384]{2,1,0:T(8,128)(2,1)}), bf16[64,8,384]{2,1,0:T(8,128)(2,1)S(1)}, u32[]{:S(2)}, u32[]{:S(2)}) async-start(bf16[64,8,384]{2,1,0:T(8,128)(2,1)} %bitcast.118), calls=%async_computation.5 | async-start | bytes 786432 | tf_op jit(solution)/shard_map/all_to_all | solution.py:24
  141.7 0.1 broadcast_in_dim.72
  141.8 0.1 broadcast_in_dim_reshape.11.index_ref
  141.9 10.3 %all-to-all-done.5 = bf16[64,8,384]{2,1,0:T(8,128)(2,1)S(1)} async-done(((bf16[64,8,384]{2,1,0:T(8,128)(2,1)}), bf16[64,8,384]{2,1,0:T(8,128)(2,1)S(1)}, u32[]{:S(2)}, u32[]{:S(2)}) %all-to-all-start.5) | async-done | bytes 393248 | tf_op jit(solution)/shard_map/all_to_all | solution.py:24
  152.2 0.7 copy-done.12
  152.9 1.1 shard_map.176
  154.0 17.5 %all_to_all.60 = bf16[64,8,512]{2,1,0:T(8,128)(2,1)S(1)} all-to-all(bf16[64,8,512]{2,1,0:T(8,128)(2,1)} %bitcast.106), channel_id=1, replica_groups=mesh['table'=64,'rep'=4] {'table'}, dimensions={0} | all-to-all | bytes 1048576 | tf_op jit(solution)/shard_map/all_to_all | solution.py:24
  171.5 1.4 shard_map.177
  172.9 28.4 %all_to_all.61 = bf16[4,368,256]{2,1,0:T(8,128)(2,1)S(1)} all-to-all(bf16[4,368,256]{2,1,0:T(8,128)(2,1)} %bitcast.104), channel_id=1, replica_groups=mesh['table'=64,'rep'=4] {'rep'}, dimensions={0} | all-to-all | bytes 1507328 | tf_op jit(solution)/shard_map/all_to_all | solution.py:367
  201.3 1.0 shard_map.178
  202.2 3.5 %all-to-all-start.8 = ((bf16[4,368,256]{2,1,0:T(8,128)(2,1)}), bf16[4,368,256]{2,1,0:T(8,128)(2,1)S(1)}, u32[]{:S(2)}, u32[]{:S(2)}) async-start(bf16[4,368,256]{2,1,0:T(8,128)(2,1)} %bitcast.103), calls=%async_computation.8 | async-start | bytes 1507328 | tf_op jit(solution)/shard_map/all_to_all | solution.py:369
  205.7 1.1 fusion.2
  206.9 18.6 %all-to-all-done.8 = bf16[4,368,256]{2,1,0:T(8,128)(2,1)S(1)} async-done(((bf16[4,368,256]{2,1,0:T(8,128)(2,1)}), bf16[4,368,256]{2,1,0:T(8,128)(2,1)S(1)}, u32[]{:S(2)}, u32[]{:S(2)}) %all-to-all-start.8) | async-done | bytes 753696 | tf_op jit(solution)/shard_map/all_to_all | solution.py:369
  225.5 1.2 shard_map.179
  226.7 1.3 slice.51
  228.0 0.8 slice.52
  228.8 0.7 reshape.245
  (70 shorter events, 0.5 us)
Async XLA Ops:
  0.6 13.5 %copy-start.19 = (s32[256]{0:T(256)S(1)}, s32[256]{0:T(256)}, u32[]{:S(2)}) copy-start(s32[256]{0:T(256)} %param.13) | copy-start | bytes 3076
  0.6 1.0 copy-start
  1.7 0.9 copy-start.3
  2.6 0.9 copy-start.8
  3.5 10.6 %copy-start.20 = (s32[256]{0:T(256)S(1)}, s32[256]{0:T(256)}, u32[]{:S(2)}) copy-start(s32[256]{0:T(256)} %param.17) | copy-start | bytes 3076
  3.5 38.1 %copy-start.1 = (bf16[512,512]{1,0:T(8,128)(2,1)S(1)}, bf16[512,512]{1,0:T(8,128)(2,1)}, u32[]{:S(2)}) copy-start(bf16[512,512]{1,0:T(8,128)(2,1)} %pooled_ref.7) | copy-start | bytes 1572868
  3.6 38.1 %copy-start.5 = (bf16[256,512]{1,0:T(8,128)(2,1)S(1)}, bf16[256,512]{1,0:T(8,128)(2,1)}, u32[]{:S(2)}) copy-start(bf16[256,512]{1,0:T(8,128)(2,1)} %u_ref.3) | copy-start | bytes 786436
  3.6 38.1 %copy-start.13 = (f32[512]{0:T(512)S(1)}, f32[512]{0:T(512)}, u32[]{:S(2)}) copy-start(f32[512]{0:T(512)} %param.16) | copy-start | bytes 6148
  4.8 19.7 %all-to-all-start = ((bf16[64,8,384]{2,1,0:T(8,128)(2,1)}), bf16[64,8,384]{2,1,0:T(8,128)(2,1)S(1)}, u32[]{:S(2)}, u32[]{:S(2)}) async-start(bf16[64,8,384]{2,1,0:T(8,128)(2,1)} %bitcast.110), calls=%async_computation | async-start | bytes 786432 | tf_op jit(solution)/shard_map/all_to_all | solution.py:24
  14.6 46.4 %copy-start.17 = (bf16[2,128,128]{2,1,0:T(8,128)(2,1)S(1)}, bf16[2,128,128]{2,1,0:T(8,128)(2,1)}, u32[]{:S(2)}) copy-start(bf16[2,128,128]{2,1,0:T(8,128)(2,1)} %param.20) | copy-start | bytes 196612
  62.8 6.4 %copy-start.21 = (s32[128]{0:T(128)S(1)}, s32[128]{0:T(128)}, u32[]{:S(2)}) copy-start(s32[128]{0:T(128)} %param.19) | copy-start | bytes 1540
  62.8 8.4 %copy-start.18 = (f32[3,4096]{1,0:T(4,128)S(1)}, f32[3,4096]{1,0:T(4,128)}, u32[]{:S(2)}) copy-start(f32[3,4096]{1,0:T(4,128)} %param.21) | copy-start | bytes 147460
  62.8 35.9 %all-to-all-start.3 = ((bf16[32,2,128,128]{3,2,1,0:T(8,128)(2,1)}), bf16[32,2,128,128]{3,2,1,0:T(8,128)(2,1)}, u32[]{:S(2)}, u32[]{:S(2)}) async-start(bf16[32,2,128,128]{3,2,1,0:T(8,128)(2,1)} %broadcast_in_dim.67), calls=%async_computation.3 | async-start | bytes 4194304 | tf_op jit(solution)/shard_map/all_to_all | solution.py:297
  72.4 1.5 collective-permute-start
  74.7 28.0 %copy-start.22 = (s32[1,8]{1,0:T(1,128)S(1)}, s32[1,8]{1,0:T(1,128)}, u32[]{:S(2)}) copy-start(s32[1,8]{1,0:T(1,128)} %param.22) | copy-start | bytes 100
  74.7 27.9 %copy-start.23 = (s32[1,8]{1,0:T(1,128)S(1)}, s32[1,8]{1,0:T(1,128)}, u32[]{:S(2)}) copy-start(s32[1,8]{1,0:T(1,128)} %param.23) | copy-start | bytes 100
  101.0 1.4 collective-permute-start.1
  102.8 1.3 collective-permute-start.2
  104.2 3.7 %copy-start.14 = (bf16[256,128]{1,0:T(8,128)(2,1)S(1)}, bf16[256,128]{1,0:T(8,128)(2,1)}, u32[]{:S(2)}) copy-start(bf16[256,128]{1,0:T(8,128)(2,1)} %get-tuple-element.25) | copy-start | bytes 196612
  104.3 4.8 %copy-start.16 = (f32[256,128]{1,0:T(8,128)S(1)}, f32[256,128]{1,0:T(8,128)}, u32[]{:S(2)}) copy-start(f32[256,128]{1,0:T(8,128)} %get-tuple-element.26) | copy-start | bytes 393220
  107.6 1.4 collective-permute-start.3
  110.1 23.2 %copy-start.2 = (f32[512,512]{1,0:T(8,128)S(1)}, f32[512,512]{1,0:T(8,128)}, u32[]{:S(2)}) copy-start(f32[512,512]{1,0:T(8,128)} %get-tuple-element.29.factor_ref) | copy-start | bytes 3145732
  110.1 23.2 %copy-start.6 = (bf16[512,512]{1,0:T(8,128)(2,1)S(1)}, bf16[512,512]{1,0:T(8,128)(2,1)}, u32[]{:S(2)}) copy-start(bf16[512,512]{1,0:T(8,128)(2,1)} %get-tuple-element.28.lifted_ref) | copy-start | bytes 1572868
  110.1 23.2 %copy-start.9 = (bf16[512,128]{1,0:T(8,128)(2,1)S(1)}, bf16[512,128]{1,0:T(8,128)(2,1)}, u32[]{:S(2)}) copy-start(bf16[512,128]{1,0:T(8,128)(2,1)} %get-tuple-element.27.weight_ref) | copy-start | bytes 393220
  135.9 35.6 %copy-start.7 = (bf16[256,512]{1,0:T(8,128)(2,1)S(1)}, bf16[256,512]{1,0:T(8,128)(2,1)}, u32[]{:S(2)}) copy-start(bf16[256,512]{1,0:T(8,128)(2,1)} %get-tuple-element.33.up_ref) | copy-start | bytes 786436
  135.9 35.6 %copy-start.10 = (bf16[256,128]{1,0:T(8,128)(2,1)S(1)}, bf16[256,128]{1,0:T(8,128)(2,1)}, u32[]{:S(2)}) copy-start(bf16[256,128]{1,0:T(8,128)(2,1)} %get-tuple-element.34.two_ref) | copy-start | bytes 196612
  135.9 35.6 %copy-start.11 = (f32[8,128]{1,0:T(8,128)S(1)}, f32[8,128]{1,0:T(8,128)}, u32[]{:S(2)}) copy-start(f32[8,128]{1,0:T(8,128)} %get-tuple-element.35.bias_ref) | copy-start | bytes 12292
  135.9 16.3 %all-to-all-start.5 = ((bf16[64,8,384]{2,1,0:T(8,128)(2,1)}), bf16[64,8,384]{2,1,0:T(8,128)(2,1)S(1)}, u32[]{:S(2)}, u32[]{:S(2)}) async-start(bf16[64,8,384]{2,1,0:T(8,128)(2,1)} %bitcast.118), calls=%async_computation.5 | async-start | bytes 786432 | tf_op jit(solution)/shard_map/all_to_all | solution.py:24
  152.2 0.7 copy-start.12
  172.9 32.9 %copy-start.4 = (bf16[512,256]{1,0:T(8,128)(2,1)S(1)}, bf16[512,256]{1,0:T(8,128)(2,1)}, u32[]{:S(2)}) copy-start(bf16[512,256]{1,0:T(8,128)(2,1)} %v_ref.1) | copy-start | bytes 786436
  172.9 32.9 %copy-start.15 = (f32[512,512]{1,0:T(8,128)S(1)}, f32[512,512]{1,0:T(8,128)}, u32[]{:S(2)}) copy-start(f32[512,512]{1,0:T(8,128)} %get-tuple-element.30) | copy-start | bytes 3145732
  202.2 23.3 %all-to-all-start.8 = ((bf16[4,368,256]{2,1,0:T(8,128)(2,1)}), bf16[4,368,256]{2,1,0:T(8,128)(2,1)S(1)}, u32[]{:S(2)}, u32[]{:S(2)}) async-start(bf16[4,368,256]{2,1,0:T(8,128)(2,1)} %bitcast.103), calls=%async_computation.8 | async-start | bytes 1507328 | tf_op jit(solution)/shard_map/all_to_all | solution.py:369
